TPU v7x, 128 devices: a whole 4x4x4 slice. The times are simulated.
128 devices in a mesh: au: 16 (over y, z), vert: 8 (over x, core).
Axes of the slice: x: 4, y: 4, z: 4, core: 2. Of those that a mesh axis runs over, the one named last changes fastest.
Arguments:
- visibilities: bfloat16 [2048, 2, 2, 256], P(('au', 'vert')), may hold values from -6 to 6
- keep_flags: int32 [2048, 256], P(('au', 'vert')), may hold values 0 or 1
- kernel_index: int32 [2048, 256], P(('au', 'vert')), may hold values from 0 to 31
- row_offset: int32 [2048, 256], P(('au', 'vert')), may hold values from 0 to 127
- col_offset: int32 [2048, 256], P(('au', 'vert')), may hold values from 0 to 127
- cell_index: int32 [2048], P(('au', 'vert')), may hold values from 0 to 31
- tile_row: int32 [2048, 1], P(('au', 'vert')), may hold values from 0 to 15; in each aligned block of 16 rows (0 to 15, 16 to 31, ...) at most 2 rows name the same one
- kernel_taps: float32 [32, 2, 16], replicated, may hold values from -1 to 1
Outputs:
- dirty_gradient: float32 [2, 8192, 8192], P(None, ('au', 'vert'))
Inputs may be any that keep to these rules, and one draw needn't show every extreme that they name: `tile_row`: of one device's 16 blocks at most 2 name the same tile row, and in every draw some device has exactly 2 for some tile row.
All inputs are finite; a program needn't handle non-finite values. No bound on the sum of `keep_flags` on one device may be relied on, other than what follows from the above.
Results may differ from a plain program's by a relative error of at most 0.0041.
Values may be sent and summed in bfloat16 or wider, within the bound.
A program may use at most 192 MiB of HBM per device.

v0:
```python
import math

import jax
import jax.numpy as jnp
from jax import lax
from jax.sharding import PartitionSpec as P

KVIS = 256
TAPS = 16
WPLANES = 32
CELL = 128
TILE_R = 512
TILE_C = 1024
NB_DEV = 16


exact_mode = lax.Precision.HIGHEST


def shifted(block, axis, distance):
    devices = range(lax.axis_size(axis))
    route = [(i - distance, i) for i in devices if i - distance in devices]
    return lax.ppermute(block, axis, route)


def weighted_taps(masked, kernel_index, kernel_taps):
    wplane_count = kernel_taps.shape[0]
    selector = (kernel_index[..., None] == jnp.arange(wplane_count, dtype=jnp.int32)).astype(
        jnp.float32
    )
    taps_full = jnp.einsum("bkw,wct->bckt", selector, kernel_taps, precision=exact_mode)
    values = masked.astype(jnp.float32)
    real_vis = values[:, :, 0, :, None]
    imag_vis = values[:, :, 1, :, None]
    real_tap = taps_full[:, None, 0]
    imag_tap = taps_full[:, None, 1]
    weighted = jnp.stack(
        [real_vis * real_tap - imag_vis * imag_tap, real_vis * imag_tap + imag_vis * real_tap],
        axis=2,
    )
    return (weighted.astype(jnp.bfloat16), taps_full.astype(jnp.bfloat16))


def make_patches(weighted, taps, row_pos, col_pos, patch_size):
    tap_count = taps.shape[-1]
    span_idx = jnp.arange(patch_size, dtype=jnp.int32)
    tap_steps = jnp.arange(tap_count, dtype=jnp.int32)
    row_hit = (row_pos[:, :, None, None] + tap_steps[None, None, :, None] == span_idx).astype(
        jnp.bfloat16
    )
    col_hit = (col_pos[:, :, None, None] + tap_steps[None, None, :, None] == span_idx).astype(
        jnp.bfloat16
    )
    row_kernel = jnp.einsum(
        "bpckt,bkta->bpcka", weighted, row_hit, preferred_element_type=jnp.float32
    ).astype(jnp.bfloat16)
    col_kernel = jnp.einsum(
        "bdkt,bktl->bdkl", taps, col_hit, preferred_element_type=jnp.float32
    ).astype(jnp.bfloat16)
    products = jnp.einsum(
        "bpcka,bdkl->bpcdal", row_kernel, col_kernel, preferred_element_type=jnp.float32
    )
    real_part = products[:, :, 0, 0] - products[:, :, 1, 1]
    imag_part = products[:, :, 0, 1] + products[:, :, 1, 0]
    return jnp.stack([real_part, imag_part], axis=2)


def dft_last(real_in, imag_in, want_imag):
    length = real_in.shape[-1]
    short_len = min(128, length)
    long_len = length // short_len
    leading = real_in.shape[:-1]
    real_in = real_in.reshape(leading + (long_len, short_len))
    imag_in = imag_in.reshape(leading + (long_len, short_len))
    outer_idx = jnp.arange(long_len, dtype=jnp.int32)
    inner_idx = jnp.arange(short_len, dtype=jnp.int32)
    angle_one = (
        2.0
        * math.pi
        / long_len
        * (outer_idx[:, None] * outer_idx[None, :] % long_len).astype(jnp.float32)
    )
    cosine_one = jnp.cos(angle_one)
    sine_one = jnp.sin(angle_one)
    real_mid = jnp.einsum(
        "...ab,aq->...qb", real_in, cosine_one, precision=exact_mode
    ) - jnp.einsum("...ab,aq->...qb", imag_in, sine_one, precision=exact_mode)
    imag_mid = jnp.einsum("...ab,aq->...qb", real_in, sine_one, precision=exact_mode) + jnp.einsum(
        "...ab,aq->...qb", imag_in, cosine_one, precision=exact_mode
    )
    angle_two = (
        2.0
        * math.pi
        / length
        * (outer_idx[:, None] * inner_idx[None, :] % length).astype(jnp.float32)
    )
    cosine_two = jnp.cos(angle_two)
    sine_two = jnp.sin(angle_two)
    real_turned = real_mid * cosine_two - imag_mid * sine_two
    imag_turned = real_mid * sine_two + imag_mid * cosine_two
    angle_three = (
        2.0
        * math.pi
        / short_len
        * (inner_idx[:, None] * inner_idx[None, :] % short_len).astype(jnp.float32)
    )
    cosine_three = jnp.cos(angle_three)
    sine_three = jnp.sin(angle_three)
    real_out = jnp.einsum(
        "...qb,bk->...kq", real_turned, cosine_three, precision=exact_mode
    ) - jnp.einsum("...qb,bk->...kq", imag_turned, sine_three, precision=exact_mode)
    real_out = real_out.reshape(leading + (length,))
    if want_imag:
        imag_out = jnp.einsum(
            "...qb,bk->...kq", real_turned, sine_three, precision=exact_mode
        ) + jnp.einsum("...qb,bk->...kq", imag_turned, cosine_three, precision=exact_mode)
        return (real_out, imag_out.reshape(leading + (length,)))
    return (real_out, real_out)


def shards(
    visibilities,
    keep_flags,
    kernel_index,
    row_offset,
    col_offset,
    cell_index,
    tile_row,
    kernel_taps,
):
    plane_count = visibilities.shape[1]
    vis_count = visibilities.shape[3]
    tap_count = kernel_taps.shape[2]
    rows_count = lax.axis_size("au")
    columns_count = lax.axis_size("vert")
    capacity = max(2, 2 * NB_DEV // rows_count)
    slot_count = rows_count * capacity
    cells_across = TILE_C // CELL
    cells_down = TILE_R // CELL
    cell_total = cells_down * cells_across
    patch_size = CELL + TAPS
    masked = jnp.where(
        keep_flags[:, None, None, :] == 1, visibilities, jnp.zeros_like(visibilities)
    )
    packed = (
        (cell_index[:, None] * CELL + row_offset) * CELL + col_offset
    ) * WPLANES + kernel_index
    target = tile_row[:, 0]
    block_ids = jnp.arange(NB_DEV, dtype=jnp.int32)
    earlier = (target[None, :] == target[:, None]) & (block_ids[None, :] < block_ids[:, None])
    rank_in = jnp.sum(earlier.astype(jnp.int32), axis=1)
    slot_of = target * capacity + rank_in
    chosen = (slot_of[None, :] == jnp.arange(slot_count, dtype=jnp.int32)[:, None]).astype(
        jnp.int32
    )
    present = jnp.sum(chosen, axis=1)
    source = jnp.sum(chosen * block_ids[None, :], axis=1)

    def to_slots(values):
        picked = jnp.take(values, source, axis=0)
        keep_mask = present.reshape((slot_count,) + (1,) * (values.ndim - 1))
        return jnp.where(keep_mask == 1, picked, jnp.zeros_like(picked))

    packed_slots = to_slots(packed).reshape(rows_count, capacity, vis_count)
    masked_slots = to_slots(masked).reshape(rows_count, capacity, plane_count, 2, vis_count)
    got_masked, got_codes = (
        lax.all_to_all(masked_slots, "au", split_axis=0, concat_axis=0, tiled=True),
        lax.all_to_all(packed_slots, "au", split_axis=0, concat_axis=0, tiled=True),
    )
    codes_all = got_codes.reshape(slot_count, vis_count)
    weighted_all, taps_all = weighted_taps(
        got_masked.reshape(slot_count, plane_count, 2, vis_count), codes_all % WPLANES, kernel_taps
    )
    group_size = math.gcd(slot_count, 8)
    group_count = slot_count // group_size

    def grid_group(cell_sums, group):
        weighted_group, taps_group, codes_group = group
        position = codes_group // WPLANES
        col_pos = position % CELL
        row_pos = position // CELL % CELL
        cells_group = position[:, 0] // (CELL * CELL)
        patches = make_patches(weighted_group, taps_group, row_pos, col_pos, patch_size)
        return (cell_sums.at[cells_group].add(patches), None)

    start_sums = jnp.zeros((cell_total, plane_count, 2, patch_size, patch_size), jnp.float32)
    cell_sums = lax.scan(
        grid_group,
        start_sums,
        (
            weighted_all.reshape(group_count, group_size, plane_count, 2, vis_count, tap_count),
            taps_all.reshape(group_count, group_size, 2, vis_count, tap_count),
            codes_all.reshape(group_count, group_size, vis_count),
        ),
    )[0]
    arranged = cell_sums.reshape(
        cells_down, cells_across, plane_count, 2, patch_size, patch_size
    ).transpose(2, 3, 0, 4, 1, 5)
    main_part = arranged[:, :, :, :CELL, :, :CELL].reshape(plane_count, 2, TILE_R, TILE_C)
    right_part = jnp.pad(
        arranged[:, :, :, :CELL, :, CELL:],
        ((0, 0), (0, 0), (0, 0), (0, 0), (0, 0), (0, CELL - TAPS)),
    ).reshape(plane_count, 2, TILE_R, TILE_C)
    lower_part = jnp.pad(
        arranged[:, :, :, CELL:, :, :CELL],
        ((0, 0), (0, 0), (0, 0), (0, CELL - TAPS), (0, 0), (0, 0)),
    ).reshape(plane_count, 2, TILE_R, TILE_C)
    corner_part = jnp.pad(
        arranged[:, :, :, CELL:, :, CELL:],
        ((0, 0), (0, 0), (0, 0), (0, CELL - TAPS), (0, 0), (0, CELL - TAPS)),
    ).reshape(plane_count, 2, TILE_R, TILE_C)
    extended = jnp.zeros((plane_count, 2, TILE_R + CELL, TILE_C + CELL), jnp.float32)
    extended = extended.at[:, :, :TILE_R, :TILE_C].add(main_part)
    extended = extended.at[:, :, :TILE_R, CELL:].add(right_part)
    extended = extended.at[:, :, CELL:, :TILE_C].add(lower_part)
    extended = extended.at[:, :, CELL:, CELL:].add(corner_part)
    side_strip = extended[:, :, : TILE_R + TAPS, TILE_C : TILE_C + TAPS]
    from_left = shifted(side_strip.astype(jnp.bfloat16), "vert", 1).astype(side_strip.dtype)
    tile_grid = extended[:, :, : TILE_R + TAPS, :TILE_C]
    tile_grid = tile_grid.at[:, :, :, :TAPS].add(from_left)
    low_strip = tile_grid[:, :, TILE_R:, :]
    from_above = shifted(low_strip, "au", 1)
    tile_grid = tile_grid[:, :, :TILE_R, :].at[:, :, :TAPS, :].add(from_above)
    stacked = tile_grid.reshape(plane_count * 2, TILE_R, TILE_C)
    wide_rows = lax.all_to_all(stacked, "vert", split_axis=1, concat_axis=2, tiled=True)
    row_share = wide_rows.shape[1]
    grid_cols = wide_rows.shape[2]
    real_cols, imag_cols = dft_last(wide_rows[0::2], wide_rows[1::2], True)
    turned = jnp.stack([real_cols, imag_cols], axis=1).reshape(
        plane_count * 2, row_share, grid_cols
    )
    tall_cols = lax.all_to_all(turned, ("au", "vert"), split_axis=2, concat_axis=1, tiled=True)
    flipped = jnp.swapaxes(tall_cols, 1, 2)
    real_image = dft_last(flipped[0::2], flipped[1::2], False)[0]
    scale = 1.0 / math.sqrt(NB_DEV * rows_count * columns_count * KVIS)
    return real_image * scale


def solution(mesh):
    in_specs = (
        P(("au", "vert"), None, None, None),
        P(("au", "vert"), None),
        P(("au", "vert"), None),
        P(("au", "vert"), None),
        P(("au", "vert"), None),
        P(("au", "vert")),
        P(("au", "vert"), None),
        P(),
    )
    out_specs = P(None, ("au", "vert"), None)
    return jax.shard_map(shards, mesh=mesh, in_specs=in_specs, out_specs=out_specs, check_vma=False)
```

profile of v0, /device:TPU:1, one launch (start us, length us, event | category | flops | bytes accessed | tf_op | source)
XLA Modules:
  0.0 899.0 jit_solution(8921534277940100933)
XLA Ops:
  4.7 8.6 all-to-all-start
  32.4 8.8 broadcast_in_dim.59
  41.3 182.8 %while.19 = (s32[]{:T(128)}, f32[32,2,2,144,144]{4,3,2,1,0:T(8,128)}, s32[4,8,256]{2,1,0:T(8,128)S(1)}, bf16[4,8,2,256,16]{3,4,2,1,0:T(8,128)(2,1)}, bf16[4,8,2,2,256,16]{4,5,3,2,1,0:T(8,128)(2,1)S(1)}, /*index=5*/s32[]{:T(128)}) while((s32[]{:T(128)}, f32[32,2,2,144,144]{4,3,2,1,0:T(8,128)}, s32[4,8,256]{2,1,0:T(8,128)S(1)}, ...), condition=%wide.region_5.6_spmd, body=%wide.region_3.5_spmd.sunk | while | flops 749455488 | bytes 59621692 | solution.py:187
  44.3 10.8 %fusion.229 = bf16[8,2,2,256,144,1]{4,2,1,3,0,5:T(2,128)(2,1)} fusion(s32[8,256,16]{2,1,0:T(8,128)S(1)} %iota_add_fusion.4, bf16[1,8,2,2,256,16]{5,3,2,4,1,0:T(2,128)(2,1)S(1)} %copy.146), kind=kOutput, calls=%fused_computation.12.clone.1 | convolution fusion | flops 43646976 | bytes 2752512 | tf_op jit(solution)/shard_map/while/body/eval_jaxpr/bpckt,bkta->bpcka/dot_general | solution.py:54
  57.2 8.6 fusion.230
  77.5 9.2 %scatter_fusion = f32[32,2,2,144,144]{4,3,2,1,0:T(8,128)} fusion(f32[32,2,2,144,144]{4,3,2,1,0:T(8,128)} %get-tuple-element.268, s32[8]{0:T(128)S(1)} %fusion.228, f32[8,2,2,144,144]{4,3,2,1,0:T(8,128)} %copy.149), kind=kCustom, calls=%fused_computation.2.clone.1 | custom fusion | flops 663552 | bytes 7962656 | tf_op jit(solution)/shard_map/while/body/eval_jaxpr/scatter-add | solution.py:184
  89.7 10.8 %fusion.229 = bf16[8,2,2,256,144,1]{4,2,1,3,0,5:T(2,128)(2,1)} fusion(s32[8,256,16]{2,1,0:T(8,128)S(1)} %iota_add_fusion.4, bf16[1,8,2,2,256,16]{5,3,2,4,1,0:T(2,128)(2,1)S(1)} %copy.146), kind=kOutput, calls=%fused_computation.12.clone.1 | convolution fusion | flops 43646976 | bytes 2752512 | tf_op jit(solution)/shard_map/while/body/eval_jaxpr/bpckt,bkta->bpcka/dot_general | solution.py:54
  122.9 9.5 %scatter_fusion = f32[32,2,2,144,144]{4,3,2,1,0:T(8,128)} fusion(f32[32,2,2,144,144]{4,3,2,1,0:T(8,128)} %get-tuple-element.268, s32[8]{0:T(128)S(1)} %fusion.228, f32[8,2,2,144,144]{4,3,2,1,0:T(8,128)} %copy.149), kind=kCustom, calls=%fused_computation.2.clone.1 | custom fusion | flops 663552 | bytes 7962656 | tf_op jit(solution)/shard_map/while/body/eval_jaxpr/scatter-add | solution.py:184
  135.4 10.8 %fusion.229 = bf16[8,2,2,256,144,1]{4,2,1,3,0,5:T(2,128)(2,1)} fusion(s32[8,256,16]{2,1,0:T(8,128)S(1)} %iota_add_fusion.4, bf16[1,8,2,2,256,16]{5,3,2,4,1,0:T(2,128)(2,1)S(1)} %copy.146), kind=kOutput, calls=%fused_computation.12.clone.1 | convolution fusion | flops 43646976 | bytes 2752512 | tf_op jit(solution)/shard_map/while/body/eval_jaxpr/bpckt,bkta->bpcka/dot_general | solution.py:54
  168.6 9.5 %scatter_fusion = f32[32,2,2,144,144]{4,3,2,1,0:T(8,128)} fusion(f32[32,2,2,144,144]{4,3,2,1,0:T(8,128)} %get-tuple-element.268, s32[8]{0:T(128)S(1)} %fusion.228, f32[8,2,2,144,144]{4,3,2,1,0:T(8,128)} %copy.149), kind=kCustom, calls=%fused_computation.2.clone.1 | custom fusion | flops 663552 | bytes 7962656 | tf_op jit(solution)/shard_map/while/body/eval_jaxpr/scatter-add | solution.py:184
  181.2 10.8 %fusion.229 = bf16[8,2,2,256,144,1]{4,2,1,3,0,5:T(2,128)(2,1)} fusion(s32[8,256,16]{2,1,0:T(8,128)S(1)} %iota_add_fusion.4, bf16[1,8,2,2,256,16]{5,3,2,4,1,0:T(2,128)(2,1)S(1)} %copy.146), kind=kOutput, calls=%fused_computation.12.clone.1 | convolution fusion | flops 43646976 | bytes 2752512 | tf_op jit(solution)/shard_map/while/body/eval_jaxpr/bpckt,bkta->bpcka/dot_general | solution.py:54
  214.4 9.7 %scatter_fusion = f32[32,2,2,144,144]{4,3,2,1,0:T(8,128)} fusion(f32[32,2,2,144,144]{4,3,2,1,0:T(8,128)} %get-tuple-element.268, s32[8]{0:T(128)S(1)} %fusion.228, f32[8,2,2,144,144]{4,3,2,1,0:T(8,128)} %copy.149), kind=kCustom, calls=%fused_computation.2.clone.1 | custom fusion | flops 663552 | bytes 7962656 | tf_op jit(solution)/shard_map/while/body/eval_jaxpr/scatter-add | solution.py:184
  224.1 17.2 %copy.132 = f32[4,8,2,2,144,144]{5,1,4,0,3,2:T(8,128)S(1)} copy(f32[4,8,2,2,144,144]{5,4,3,2,1,0:T(8,128)} %bitcast.277) | data formatting | bytes 21233664 | tf_op jit(solution)/shard_map/reshape | solution.py:196
  249.3 9.2 %add.363 = f32[2,2,512,1024]{3,2,1,0:T(8,128)} reshape(f32[2,2,4,128,8,128]{5,4,3,2,1,0:T(8,128)} %slice.313) | data formatting | bytes 16777216 | tf_op jit(solution)/shard_map/add | solution.py:213
  266.1 9.2 %reshape.588 = f32[2,2,512,1024]{3,2,1,0:T(8,128)} reshape(f32[2,2,4,128,8,128]{5,4,3,2,1,0:T(8,128)} %pad.33) | data formatting | bytes 16777216 | tf_op jit(solution)/shard_map/reshape.165
  275.3 8.9 scatter-add.35
  288.4 9.3 %reshape.589 = f32[2,2,512,1024]{3,2,1,0:T(8,128)} reshape(f32[2,2,4,128,8,128]{5,4,3,2,1,0:T(8,128)} %pad.34) | data formatting | bytes 16777216 | tf_op jit(solution)/shard_map/reshape.179
  301.8 9.3 %reshape.590 = f32[2,2,512,1024]{3,2,1,0:T(8,128)} reshape(f32[2,2,4,128,8,128]{5,4,3,2,1,0:T(8,128)} %pad.35) | data formatting | bytes 16777216 | tf_op jit(solution)/shard_map/reshape.193
  311.1 13.2 %add_select_fusion.4 = f32[2,2,512,1024]{3,2,1,0:T(8,128)} fusion(f32[2,2,512,1024]{3,2,1,0:T(8,128)} %reshape.588, s32[]{:T(128)} %bitcast.36, s32[]{:T(128)} %bitcast.37, pred[]{:T(512)} %and_reduce_fusion, f32[2,2,512,1024]{3,2,1,0:T(8,128)} %add.363), kind=kLoop, calls=%fused_computation.61 | loop fusion | flops 4194304 | bytes 25165832 | tf_op jit(solution)/shard_map/select.7
  324.3 45.8 %scatter-add.42 = f32[2,2,640,1152]{3,2,1,0:T(8,128)} dynamic-update-slice(f32[2,2,640,1152]{3,2,1,0:T(8,128)} %scatter-add.35, f32[2,2,512,1024]{3,2,1,0:T(8,128)} %add_select_fusion.4, s32[]{:T(128)} %constant.388.clone.1, s32[]{:T(128)} %constant.388.clone.1, s32[]{:T(128)} %bitcast.36, s32[]{:T(128)} %bitcast.37) | dynamic-update-slice | bytes 16777220 | tf_op jit(solution)/shard_map/scatter-add | solution.py:214
  370.1 12.2 %fusion.33 = f32[2,2,640,1152]{3,2,1,0:T(8,128)} fusion(f32[2,2,640,1152]{3,2,1,0:T(8,128)} %scatter-add.42, f32[2,2,512,1024]{3,2,1,0:T(8,128)} %reshape.589), kind=kLoop, calls=%fused_computation.65 | loop fusion | flops 2097152 | bytes 25165824 | tf_op jit(solution)/shard_map/scatter-add | solution.py:215
  382.3 12.1 %fusion.32 = f32[2,2,640,1152]{3,2,1,0:T(8,128)} fusion(f32[2,2,640,1152]{3,2,1,0:T(8,128)} %fusion.33, f32[2,2,512,1024]{3,2,1,0:T(8,128)} %reshape.590), kind=kLoop, calls=%fused_computation.63 | loop fusion | flops 2097152 | bytes 25165824 | tf_op jit(solution)/shard_map/scatter-add | solution.py:216
  412.4 9.9 %scatter-add.45 = f32[2,2,528,1024]{3,2,1,0:T(8,128)} dynamic-update-slice(f32[2,2,528,1024]{3,2,1,0:T(8,128)} %slice.319, f32[2,2,528,16]{3,2,1,0:T(8,128)S(1)} %slice_add_fusion.3, s32[]{:T(128)} %constant.388.clone.1, s32[]{:T(128)} %constant.388.clone.1, s32[]{:T(128)} %constant.388.clone.1, s32[]{:T(128)} %constant.388.clone.1) | dynamic-update-slice | bytes 270340 | tf_op jit(solution)/shard_map/scatter-add | solution.py:220
  437.0 12.0 %copy.88 = f32[4,512,1024]{2,0,1:T(4,128)} copy(f32[4,512,1024]{2,1,0:T(8,128)} %bitcast.38) | data formatting | bytes 16777216 | tf_op jit(solution)/shard_map/reshape | solution.py:224
  454.5 93.4 %all-to-all-done.2 = f32[4,512,1024]{2,0,1:T(4,128)} async-done(((f32[4,512,1024]{2,0,1:T(4,128)}), f32[4,512,1024]{2,0,1:T(4,128)}, u32[]{:S(2)}, u32[]{:S(2)}) %all-to-all-start.2) | async-done | bytes 8388640 | tf_op jit(solution)/shard_map/all_to_all | solution.py:225
  638.3 15.5 %copy.94 = f32[4,64,8192]{1,0,2:T(4,128)} copy(f32[4,64,8192]{2,1,0:T(8,128)} %bitcast.294) | data formatting | bytes 16777216 | tf_op jit(solution)/shard_map/reshape | solution.py:229
  653.8 20.3 %reshape.631 = f32[128,1,16384]{2,1,0:T(1,128)} reshape(f32[8192,4,64]{2,1,0:T(4,128)} %bitcast.282) | data formatting | bytes 16777216
  674.0 103.6 %all_to_all.46 = f32[128,1,16384]{2,1,0:T(1,128)} all-to-all(f32[128,1,16384]{2,1,0:T(1,128)} %reshape.631), channel_id=1, replica_groups=mesh['au'=16,'vert'=8] {'au','vert'}, dimensions={0} | all-to-all | bytes 16777216 | tf_op jit(solution)/shard_map/all_to_all | solution.py:232
  778.1 25.2 %reduce.18 = f32[128,16384]{1,0:T(8,128)} reduce(f32[128,1,16384]{2,1,0:T(1,128)} %all_to_all.46, f32[]{:T(128)} %broadcast.843), dimensions={1}, to_apply=%all_to_all.38.reduce_sub_computation | reduce | bytes 16777220 | tf_op jit(solution)/shard_map/all_to_all | solution.py:232
  803.3 15.8 %reshape.632 = f32[8192,4,64]{2,1,0:T(4,128)} reshape(f32[128,16384]{1,0:T(8,128)} %reduce.18) | data formatting | bytes 16777216
  819.1 17.7 %copy.133 = f32[4,64,128,64]{1,2,3,0:T(8,128)} copy(f32[4,64,128,64]{1,0,3,2:T(4,128)} %bitcast.283) | data formatting | bytes 16777216 | tf_op jit(solution)/shard_map/all_to_all | solution.py:232
  836.8 14.8 %all_to_all.41 = f32[4,8192,64]{1,2,0:T(8,128)} reshape(f32[4,128,64,64]{2,1,3,0:T(8,128)} %bitcast.284) | data formatting | bytes 16777216 | tf_op jit(solution)/shard_map/all_to_all | solution.py:232
  (206 shorter events, 316.0 us)
Async XLA Ops:
  0.0 25.2 %copy-start = (f32[32,2,16]{0,2,1:T(8,128)S(1)}, f32[32,2,16]{0,2,1:T(8,128)}, u32[]{:S(2)}) copy-start(f32[32,2,16]{0,2,1:T(8,128)} %param.29) | copy-start | bytes 12292
  4.7 15.1 %all-to-all-start = ((s32[16,2,256]{2,1,0:T(2,128)}), s32[16,2,256]{2,1,0:T(2,128)S(1)}, u32[]{:S(2)}, u32[]{:S(2)}) async-start(s32[16,2,256]{2,1,0:T(2,128)} %select_select_fusion), calls=%async_computation | async-start | bytes 65536 | tf_op jit(solution)/shard_map/all_to_all | solution.py:168
  19.8 11.8 %all-to-all-start.1 = ((bf16[16,2,2,2,256]{4,3,2,1,0:T(2,128)(2,1)}), bf16[16,2,2,2,256]{4,3,2,1,0:T(2,128)(2,1)S(1)}, u32[]{:S(2)}, u32[]{:S(2)}) async-start(bf16[16,2,2,2,256]{4,3,2,1,0:T(2,128)(2,1)} %broadcast_select_fusion.1), calls=%async_computation.1 | async-start | bytes 131072 | tf_op jit(solution)/shard_map/all_to_all | solution.py:167
  41.3 1.5 copy-start.5
  41.3 1.5 copy-start.7
  57.2 8.6 copy-start.2
  77.4 9.2 %copy-start.6 = (bf16[4,8,2,2,256,16]{4,5,3,2,1,0:T(8,128)(2,1)S(1)}, bf16[4,8,2,2,256,16]{4,5,3,2,1,0:T(8,128)(2,1)}, u32[]{:S(2)}) copy-start(bf16[4,8,2,2,256,16]{4,5,3,2,1,0:T(8,128)(2,1)} %copy-done.5) | copy-start | bytes 3145732 | tf_op jit(solution)/shard_map/while
  77.4 9.2 %copy-start.8 = (s32[4,8,256]{2,1,0:T(8,128)S(1)}, s32[4,8,256]{2,1,0:T(8,128)}, u32[]{:S(2)}) copy-start(s32[4,8,256]{2,1,0:T(8,128)} %copy-done.7) | copy-start | bytes 98308 | tf_op jit(solution)/shard_map/while
  86.7 1.5 copy-start.5
  86.7 1.5 copy-start.7
  102.6 8.6 copy-start.2
  122.9 9.6 %copy-start.6 = (bf16[4,8,2,2,256,16]{4,5,3,2,1,0:T(8,128)(2,1)S(1)}, bf16[4,8,2,2,256,16]{4,5,3,2,1,0:T(8,128)(2,1)}, u32[]{:S(2)}) copy-start(bf16[4,8,2,2,256,16]{4,5,3,2,1,0:T(8,128)(2,1)} %copy-done.5) | copy-start | bytes 3145732 | tf_op jit(solution)/shard_map/while
  122.9 9.6 %copy-start.8 = (s32[4,8,256]{2,1,0:T(8,128)S(1)}, s32[4,8,256]{2,1,0:T(8,128)}, u32[]{:S(2)}) copy-start(s32[4,8,256]{2,1,0:T(8,128)} %copy-done.7) | copy-start | bytes 98308 | tf_op jit(solution)/shard_map/while
  132.4 1.5 copy-start.5
  132.4 1.5 copy-start.7
  148.3 8.6 copy-start.2
  168.6 9.6 %copy-start.6 = (bf16[4,8,2,2,256,16]{4,5,3,2,1,0:T(8,128)(2,1)S(1)}, bf16[4,8,2,2,256,16]{4,5,3,2,1,0:T(8,128)(2,1)}, u32[]{:S(2)}) copy-start(bf16[4,8,2,2,256,16]{4,5,3,2,1,0:T(8,128)(2,1)} %copy-done.5) | copy-start | bytes 3145732 | tf_op jit(solution)/shard_map/while
  168.6 9.6 %copy-start.8 = (s32[4,8,256]{2,1,0:T(8,128)S(1)}, s32[4,8,256]{2,1,0:T(8,128)}, u32[]{:S(2)}) copy-start(s32[4,8,256]{2,1,0:T(8,128)} %copy-done.7) | copy-start | bytes 98308 | tf_op jit(solution)/shard_map/while
  178.2 1.5 copy-start.5
  178.2 1.5 copy-start.7
  194.1 8.6 copy-start.2
  214.4 9.7 %copy-start.6 = (bf16[4,8,2,2,256,16]{4,5,3,2,1,0:T(8,128)(2,1)S(1)}, bf16[4,8,2,2,256,16]{4,5,3,2,1,0:T(8,128)(2,1)}, u32[]{:S(2)}) copy-start(bf16[4,8,2,2,256,16]{4,5,3,2,1,0:T(8,128)(2,1)} %copy-done.5) | copy-start | bytes 3145732 | tf_op jit(solution)/shard_map/while
  214.4 9.7 %copy-start.8 = (s32[4,8,256]{2,1,0:T(8,128)S(1)}, s32[4,8,256]{2,1,0:T(8,128)}, u32[]{:S(2)}) copy-start(s32[4,8,256]{2,1,0:T(8,128)} %copy-done.7) | copy-start | bytes 98308 | tf_op jit(solution)/shard_map/while
  395.9 14.8 %collective-permute-start = (bf16[2,2,528,16]{2,3,1,0:T(8,128)(2,1)S(1)}, bf16[2,2,528,16]{2,3,1,0:T(8,128)(2,1)S(1)}, u32[]{:S(2)}, u32[]{:S(2)}) collective-permute-start(bf16[2,2,528,16]{2,3,1,0:T(8,128)(2,1)S(1)} %copy.86), channel_id=1, source_target_pairs={{0,1},{1,2},{2,3},{3,4},{4,5},{5,6},{6,7},{8,9},{9,10},{10,11},{11... | collective-permute-start | bytes 202760 | tf_op jit(solution)/shard_map/ppermute | solution.py:23
  423.2 12.1 %collective-permute-start.1 = (f32[2,2,16,1024]{3,2,1,0:T(8,128)S(1)}, f32[2,2,16,1024]{3,2,1,0:T(8,128)S(1)}, u32[]{:S(2)}, u32[]{:S(2)}) collective-permute-start(f32[2,2,16,1024]{3,2,1,0:T(8,128)S(1)} %slice.324), channel_id=1, source_target_pairs={{0,8},{8,16},{16,24},{24,32},{32,40},{40,48},{48,56},{56,64},{64,7... | collective-permute-start | bytes 786440 | tf_op jit(solution)/shard_map/ppermute | solution.py:23
  449.0 98.9 %all-to-all-start.2 = ((f32[4,512,1024]{2,0,1:T(4,128)}), f32[4,512,1024]{2,0,1:T(4,128)}, u32[]{:S(2)}, u32[]{:S(2)}) async-start(f32[4,512,1024]{2,0,1:T(4,128)} %copy.88), calls=%async_computation.2 | async-start | bytes 16777216 | tf_op jit(solution)/shard_map/all_to_all | solution.py:225
  573.2 13.9 %copy-start.3 = (f32[64,2,64,128]{3,0,2,1:T(8,128)}, f32[64,2,64,128]{3,0,2,1:T(8,128)S(1)}, u32[]{:S(2)}) copy-start(f32[64,2,64,128]{3,0,2,1:T(8,128)S(1)} %fusion.72) | copy-start | bytes 12582916
  577.7 9.3 %copy-start.4 = (f32[64,2,64,128]{3,0,2,1:T(8,128)}, f32[64,2,64,128]{3,0,2,1:T(8,128)S(1)}, u32[]{:S(2)}) copy-start(f32[64,2,64,128]{3,0,2,1:T(8,128)S(1)} %fusion.75) | copy-start | bytes 12582916
  884.0 14.8 %copy-start.1 = (f32[32,2,16]{0,2,1:T(8,128)S(1)}, f32[32,2,16]{0,2,1:T(8,128)}, u32[]{:S(2)}) copy-start(f32[32,2,16]{0,2,1:T(8,128)} %param.29) | copy-start | bytes 12292
where the time goes:
time: 912 us; the launch traced here: 899 us
  local copies, waits for them, and re-layouts  374 us (41%)
  matrix products  152 us (17%)
  other arithmetic  139 us (15%)
  blocking collectives  104 us (11%)
  waiting for transfers between devices  99.7 us (11%)
  starting transfers between devices  29.3 us (3%)
    all_to_all x1, blocking collectives, shards(): lax.all_to_all(turned, ('au', 'vert'), split_axis=2, concat_axis=1, tiled...  104 us
    all_to_all x1, waiting for transfers between devices, shards(): lax.all_to_all(stacked, 'vert', split_axis=1, concat_axis=2, tiled=True)  93.4 us
    scatter-add x1, local copies, waits for them, and re-layouts, shards(): extended = extended.at[:, :, :TILE_R, CELL:].add(right_part)  45.8 us
    dot_general x4, matrix products, make_patches(): jnp.einsum('bpckt,bkta->bpcka', weighted, row_hit, preferred_element_type...  43.3 us
    unnamed x16, local copies, waits for them, and re-layouts  39.1 us
    scatter-add x4, other arithmetic, grid_group(): return (cell_sums.at[cells_group].add(patches), None)  38 us
    dot_general x4, matrix products, make_patches(): jnp.einsum('bdkt,bktl->bdkl', taps, col_hit, preferred_element_type=jnp.f...  34.4 us
    all_to_all x3, local copies, waits for them, and re-layouts, shards(): lax.all_to_all(turned, ('au', 'vert'), split_axis=2, concat_axis=1, tiled...  33 us
  transfers between devices with their start and end apart: 5, of which 3 were waited for; matrix products, arithmetic and copies ran while one was open for 3% of the time, Pallas kernels for 0%

commit v1 on v0

v1 whole, which is shorter than its diff:
```python
import functools
import math

import jax
import jax.numpy as jnp
import numpy as np
from jax import lax
from jax.experimental import pallas as pl
from jax.experimental.pallas import tpu as pltpu
from jax.sharding import PartitionSpec as P

KVIS = 256
TAPS = 16
TILE_R = 512
TILE_C = 1024
NB_DEV = 16
BLOCKS = 2048
GRID = 8192
DEVICES = 128
ROWS = 32
HEAD = 16
WINDOW = 152
UNROLL = 4
BOTH = ("au", "vert")
F32 = jnp.float32
BF16 = jnp.bfloat16
I32 = jnp.int32
NT = (((1,), (1,)), ((), ()))
BIT_MUL = 0x077CB531


def bit_table():
    table = np.zeros(32, np.int32)
    for bit in range(32):
        table[((BIT_MUL << bit) & 0xFFFFFFFF) >> 27] = bit
    return table


def hi_lo(values):
    high = values.astype(jnp.bfloat16)
    low = (values - high.astype(np.float64)).astype(jnp.bfloat16)
    return high, low


@functools.lru_cache(None)
def column_tables():
    v0, c1 = np.arange(64), np.arange(64)
    c0 = np.arange(128)
    angle = 2 * np.pi / GRID * ((v0[None, :, None] * (128 * c1[None, None, :] + c0[:, None, None])) % GRID)
    first = np.concatenate([np.cos(angle), np.sin(angle)], axis=1)
    first = np.concatenate(hi_lo(first), axis=2)
    angle = 2 * np.pi / 128 * ((c0[:, None] * c0[None, :]) % 128)
    second = np.concatenate(hi_lo(np.concatenate([np.cos(angle), np.sin(angle)], axis=1)), axis=0)
    angle = 2 * np.pi / GRID * (v0[:, None] * c0[None, :])
    turn = np.concatenate([np.cos(angle), np.sin(angle)], axis=0).astype(np.float32)
    return first, second, turn


@functools.lru_cache(None)
def row_tables():
    scale = 1.0 / math.sqrt(BLOCKS * KVIS)
    u0, s = np.arange(256), np.arange(128)
    angle = 2 * np.pi / 256 * ((u0[:, None] * s[None, :]) % 256)
    first = np.concatenate([np.cos(angle), np.sin(angle)], axis=1).astype(jnp.bfloat16)
    comp, j = np.arange(128) // 64, np.arange(128) % 32
    plane = np.arange(128) // 32 % 2
    angle = 2 * np.pi / GRID * (u0[:, None] * j[None, :])
    turn_cos = (np.cos(angle) * scale).astype(np.float32)
    turn_sin = (np.sin(angle) * np.where(comp == 0, -1.0, 1.0) * scale).astype(np.float32)
    alternate = ((1.0 - 2.0 * (u0 % 2))[:, None] * ((comp == 0) & (j == 0))[None, :]).astype(np.float32)
    u1 = np.arange(32)
    angle = 2 * np.pi / 32 * ((u1[:, None] * j[None, :]) % 32)
    last = np.where(comp == 0, np.cos(angle), -np.sin(angle))
    last = np.concatenate([last * (plane == p) for p in range(2)], axis=0)
    last = np.concatenate(hi_lo(last), axis=1)
    return first, np.stack([turn_cos, turn_sin, alternate]), last


def iota(shape, dim):
    return lax.broadcasted_iota(I32, shape, dim)


def ones_where(mask):
    return jnp.where(mask, 1.0, 0.0).astype(BF16)


def dot(a, b):
    return jnp.dot(a, b, preferred_element_type=F32)


def dot_nt(a, b):
    return lax.dot_general(a, b, NT, preferred_element_type=F32)


def sort_kernel(x_ref, out_ref):
    below = ones_where(iota((128, 128), 1) < iota((128, 128), 0))
    before = ones_where(iota((KVIS, KVIS), 0) < iota((KVIS, KVIS), 1))
    ones = jnp.ones((KVIS, KVIS), BF16)
    value = iota((128, KVIS), 0)
    place = iota((KVIS, KVIS), 0)

    def one_block(i, carry):
        x = x_ref[i]
        row = x.astype(F32)[4:5].astype(I32)
        hit = value == row
        hot = ones_where(hit)
        rank = dot(hot, before) + dot(dot(below, hot).astype(BF16), ones)
        rank = jnp.sum(jnp.where(hit, rank, 0.0), axis=0, keepdims=True)
        moved = dot_nt(x, ones_where(place == rank.astype(I32)))
        both = jnp.concatenate([moved[:, :128], moved[:, 128:]], axis=0)
        out_ref[pl.ds(pl.multiple_of(i * 16, 16), 16), :] = both.astype(BF16)
        return carry

    lax.fori_loop(0, NB_DEV, one_block, 0, unroll=2)


def pick(halves, index, low):
    first, second = [jnp.take_along_axis(half, index, axis=0, mode="promise_in_bounds") for half in halves]
    return jnp.where(low, first, second)


def placed(sources, tap, limit):
    halves = [(source[:8], source[8:]) for source in sources]
    parts = [[] for _ in sources]
    for i in range(tap.shape[0] // 8):
        t = tap[8 * i : 8 * i + 8]
        inside = (t >= 0) & (t < limit)
        low = t < 8
        index = t & 7
        for out, pair in zip(parts, halves):
            out.append(jnp.where(inside, pick(pair, index, low), 0.0))
    return [jnp.concatenate(part, axis=0) for part in parts]


def grid_kernel(
    words, meta, bits, strip, x_ref, taps_ref, first_ref, second_ref, turn_ref,
    out_ref, acc, mid, stage, acc4, extra, items,
):
    s = strip[0]
    acc[...] = jnp.zeros_like(acc)
    acc4[...] = jnp.zeros_like(acc4)
    table = taps_ref[...]
    table_hi = table.astype(BF16)
    table_lo = (table - table_hi.astype(F32)).astype(BF16)
    both_tables = jnp.concatenate([table_hi, table_lo], axis=0)

    def listed(kind, count):
        def group(g, n):
            def step(state):
                word, n = state
                low = word & -word
                bit = bits[lax.shift_right_logical(low * BIT_MUL, 27)]
                items[n] = (kind << 12) | ((g * NB_DEV + (bit & 15)) << 1) | (bit >> 4)
                return word ^ low, n + 1

            return lax.while_loop(lambda state: state[0] != 0, step, (words[kind * 128 + g], n))[1]

        return lax.fori_loop(0, 128, group, count)

    def loaded(code):
        half, block = code & 1, (code >> 1) & (BLOCKS - 1)
        where = meta[block]
        cell = (where >> 14) & 31
        anchor_row = (where >> 19) * TILE_R + (cell >> 3) * 128
        anchor_col = ((block >> 4) & 7) * TILE_C + (cell & 7) * 128
        x = x_ref[pl.ds(pl.multiple_of(block * 16, 16), 16), :].astype(F32)
        x = jnp.where(half == 1, x[8:], x[:8])
        row, col, wplane = [x[i : i + 1].astype(I32) for i in (4, 5, 6)]
        chosen = ones_where(iota((32, 128), 0) == wplane)
        taps = dot(both_tables, chosen)
        tap_re, tap_im = taps[:16], taps[16:32]
        full_re, full_im = tap_re + taps[32:48], tap_im + taps[48:64]
        weights_re, weights_im = [], []
        for p in range(2):
            re, im = x[2 * p : 2 * p + 1], x[2 * p + 1 : 2 * p + 2]
            weights_re.append((re * full_re - im * full_im).astype(BF16).astype(F32))
            weights_im.append((re * full_im + im * full_re).astype(BF16).astype(F32))
        limit = jnp.minimum(jnp.where(anchor_col == GRID - 128, 128, 1000) - col, TAPS)
        return anchor_row, anchor_col, row, col, (tap_re, tap_im), weights_re + weights_im, limit

    def item(code, valid):
        anchor_row, anchor_col, row, col, taps, weights, limit = loaded(code)
        mirror = (code >> 12) == 1
        sign = jnp.where(mirror, -1, 1)
        base = jnp.where(mirror, GRID - s * ROWS, s * ROWS) - anchor_row
        base = jnp.where(valid, base, -100000)
        least = jnp.where(mirror & (s == 0), 1, 0)
        j = iota((ROWS, 128), 0)
        tap = jnp.where(j < least, -1, base + sign * j - row)
        re0, re1, im0, im1 = placed(weights, tap, TAPS)
        flip = jnp.where(mirror, -1.0, 1.0)
        left = jnp.concatenate([re0, re1, im0 * flip, im1 * flip], axis=0).astype(BF16)
        right = jnp.concatenate([-im0, -im1, re0 * flip, re1 * flip], axis=0).astype(BF16)
        tap = jnp.where(mirror, 144, 0) + sign * iota((WINDOW, 128), 0) - col
        col_re, col_im = placed(taps, tap, limit)
        cols = jnp.concatenate([col_re.astype(BF16), col_im.astype(BF16)], axis=1)
        patch = dot_nt(cols, jnp.concatenate([left, right], axis=1))
        start = jnp.where(mirror, GRID - 128 - anchor_col, anchor_col + HEAD)
        return pl.multiple_of(start, 16), patch

    count = listed(1, listed(0, 0))

    def several(i, carry):
        found = []
        for k in range(UNROLL):
            n = i * UNROLL + k
            valid = n < count
            found.append(item(jnp.where(valid, items[n], 0), valid))
        for start, patch in found:
            acc[pl.ds(start, WINDOW), :] += patch
        return carry

    lax.fori_loop(0, (count + UNROLL - 1) // UNROLL, several, 0)
    acc[HEAD : HEAD + 8, :] += jnp.where(iota((8, 128), 0) == 0, acc[HEAD + GRID : HEAD + GRID + 8, :], 0.0)

    count4 = listed(2, 0)

    def single(i, carry):
        anchor_row, anchor_col, row, col, taps, weights, limit = loaded(items[i])
        tap = jnp.broadcast_to(GRID // 2 - anchor_row - row, (8, 128))
        re0, re1, im0, im1 = placed(weights, tap, TAPS)
        q = iota((8, 128), 0)
        left = jnp.where(q == 0, re0, jnp.where(q == 1, re1, jnp.where(q == 2, im0, jnp.where(q == 3, im1, 0.0))))
        right = jnp.where(q == 0, -im0, jnp.where(q == 1, -im1, jnp.where(q == 2, re0, jnp.where(q == 3, re1, 0.0))))
        rows = jnp.concatenate([left, right], axis=1).astype(BF16)
        tap = iota((WINDOW, 128), 0) - col
        col_re, col_im = placed(taps, tap, limit)
        cols = jnp.concatenate([col_re, col_im], axis=1)
        tail = jnp.concatenate([cols[128:], jnp.zeros((256 - WINDOW, 256), F32)], axis=0)
        c1 = anchor_col >> 7
        acc4[pl.ds(pl.multiple_of(c1 * 8, 8), 8), :] += dot_nt(rows, cols[:128].astype(BF16))
        acc4[pl.ds(pl.multiple_of(c1 * 8 + 8, 8), 8), :] += dot_nt(rows, tail.astype(BF16))
        return carry

    lax.fori_loop(0, count4, single, 0)

    lane = iota((1, 128), 1)
    flip = jnp.where(lane < 64, -1.0, 1.0)

    @pl.when(s != 0)
    def _():
        extra[...] = jnp.zeros_like(extra)

    @pl.when(s == 0)
    def _():
        cosine = first_ref[0, :64, :64]
        sine = first_ref[0, 64:, :64]
        turn_cos, turn_sin = turn_ref[:64], turn_ref[64:]
        for p in range(2):
            re = acc4[pl.ds(p, 64, stride=8), :].astype(BF16)
            im = acc4[pl.ds(2 + p, 64, stride=8), :].astype(BF16)
            mid_re = dot(cosine, re) - dot(sine, im)
            mid_im = dot(cosine, im) + dot(sine, re)
            turned_re = (mid_re * turn_cos - mid_im * turn_sin).astype(BF16)
            turned_im = (mid_re * turn_sin + mid_im * turn_cos).astype(BF16)
            got = dot_nt(second_ref[:128, :128], turned_re) - dot_nt(second_ref[:128, 128:], turned_im)
            extra[p] = got.astype(BF16)

    def column_first(c0, carry):
        h = acc[pl.ds(HEAD + c0, 64, stride=128), :]
        high = h.astype(BF16)
        low = (h - high.astype(F32)).astype(BF16)
        factors = first_ref[c0]
        got = dot(
            jnp.concatenate([factors, factors], axis=1), jnp.concatenate([high, high, low, low], axis=0)
        )
        y = got[:64] + flip * pltpu.roll(got[64:], 64, 1)
        mid[pl.ds(pl.multiple_of(c0 * 64, 64), 64), :] = y
        return carry

    lax.fori_loop(0, 128, column_first, 0, unroll=4)

    special = (s == 0) & ((lane == 64) | (lane == 96))
    keep = jnp.where(special, 0.0, 1.0)
    second_hi = second_ref[:128]
    second_lo = second_ref[128:]
    spot = iota((64, 128), 0)
    spot_lane = iota((64, 128), 1)

    for group in range(4):

        def column_second(v, carry):
            v0 = group * 16 + v
            y = mid[pl.ds(v0, 128, stride=64), :]
            turned = flip * pltpu.roll(y, 64, 1)
            pair = jnp.concatenate([y.astype(BF16), turned.astype(BF16)], axis=0)
            z = dot(second_hi, pair) + dot(second_lo, pair)
            more = dot(extra[0], ones_where((spot == v0) & (spot_lane == 64)))
            more = more + dot(extra[1], ones_where((spot == v0) & (spot_lane == 96)))
            stage[pl.ds(v, 128, stride=16), :] = z * keep + more
            return carry

        lax.fori_loop(0, 16, column_second, 0, unroll=2)

        def pack(d, carry):
            out_ref[d, group * 16 : group * 16 + 16, :] = stage[
                pl.ds(pl.multiple_of(d * 16, 16), 16), :
            ].astype(BF16)
            return carry

        lax.fori_loop(0, 128, pack, 0, unroll=8)


def image_kernel(in_ref, first_ref, turn_ref, last_ref, out_ref, wide, left, right):
    def widen(s, carry):
        wide[pl.ds(pl.multiple_of(s * 16, 16), 16), :] = in_ref[s].astype(F32)
        return carry

    lax.fori_loop(0, DEVICES, widen, 0, unroll=8)
    flip = jnp.where(iota((1, 128), 1) < 64, -1.0, 1.0)
    first = first_ref[...]
    last = last_ref[...]

    def one(v, carry):
        y = wide[pl.ds(v, DEVICES, stride=16), :]
        rolled = pltpu.roll(y, 64, 1)
        pair = jnp.concatenate([y.astype(BF16), (flip * rolled).astype(BF16)], axis=0)
        got = dot(first, pair) + turn_ref[2] * rolled[:1]
        turned = (got * turn_ref[0] + pltpu.roll(got, 64, 1) * turn_ref[1]).astype(BF16)
        result = dot_nt(last, jnp.concatenate([turned, turned], axis=1))
        left[pl.ds(pl.multiple_of(v * 64, 64), 64), :] = result[:, :128]
        right[pl.ds(pl.multiple_of(v * 64, 64), 64), :] = result[:, 128:]
        return carry

    lax.fori_loop(0, 16, one, 0, unroll=2)

    def place(u1, carry):
        for p in range(2):
            for half in range(2):
                for side, ref in ((0, left), (1, right)):
                    out_ref[p, half * 8 : half * 8 + 8, pl.ds(pl.multiple_of(u1 * 256 + side * 128, 128), 128)] = (
                        ref[pl.ds(half * 512 + p * 32 + u1, 8, stride=64), :]
                    )
        return carry

    lax.fori_loop(0, 32, place, 0, unroll=2)


def words_of(code, s):
    row = (code >> 19) * TILE_R + ((code >> 17) & 3) * 128
    top, bottom = (code >> 7) & 127, code & 127
    shift = jnp.arange(NB_DEV, dtype=I32)[None, :]

    def packed(first, final):
        hit = (final >= 0) & (first < 128 + TAPS - 1)
        one = (hit & (top >= first - (TAPS - 1))).astype(I32)
        two = (hit & (bottom <= final)).astype(I32)
        both = one.reshape(128, NB_DEV) << shift | two.reshape(128, NB_DEV) << (shift + 16)
        return jnp.sum(both, axis=1)

    direct = s * ROWS - row
    mirror = GRID - ROWS + 1 - s * ROWS - row
    middle = GRID // 2 - row
    middle = packed(middle, middle) * (s == 0).astype(I32)
    return jnp.concatenate([packed(direct, direct + ROWS - 1), packed(mirror, mirror + ROWS - 1), middle])


def shards(visibilities, keep_flags, kernel_index, row_offset, col_offset, cell_index, tile_row, kernel_taps):
    s = lax.axis_index("au") * 8 + lax.axis_index("vert")
    masked = jnp.where(keep_flags[:, None, :] == 1, visibilities.reshape(NB_DEV, 4, KVIS), 0).astype(BF16)
    codes = jnp.stack([row_offset, col_offset, kernel_index, jnp.zeros_like(row_offset)], axis=1)
    x8 = jnp.concatenate([masked, codes.astype(BF16)], axis=1)
    vmem = pl.BlockSpec(memory_space=pltpu.VMEM)
    smem = pl.BlockSpec(memory_space=pltpu.SMEM)
    ordered = pl.pallas_call(
        sort_kernel,
        out_shape=jax.ShapeDtypeStruct((NB_DEV * 16, 128), BF16),
        in_specs=[vmem],
        out_specs=vmem,
        name="sort_blocks",
    )(x8)
    by_block = ordered.reshape(NB_DEV, 16, 128)
    top = by_block[:, 4, 127].astype(I32)
    bottom = by_block[:, 12, 0].astype(I32)
    code = ((tile_row[:, 0] * 32 + cell_index) << 14) | (top << 7) | bottom
    codes_all = lax.all_gather(code, BOTH, axis=0, tiled=True)
    x_all = lax.all_gather(ordered, BOTH, axis=0, tiled=True)
    words = words_of(codes_all, s)
    first, second, turn = column_tables()
    taps = kernel_taps.transpose(1, 2, 0).reshape(2 * TAPS, 32)
    sent = pl.pallas_call(
        grid_kernel,
        out_shape=jax.ShapeDtypeStruct((DEVICES, 64, 128), BF16),
        in_specs=[smem] * 4 + [vmem] * 5,
        out_specs=vmem,
        scratch_shapes=[
            pltpu.VMEM((HEAD + GRID + 32, 128), F32),
            pltpu.VMEM((128 * 64, 128), F32),
            pltpu.VMEM((DEVICES * 16, 128), F32),
            pltpu.VMEM((66 * 8, 128), F32),
            pltpu.VMEM((2, 128, 64), BF16),
            pltpu.SMEM((4096,), I32),
        ],
        compiler_params=pltpu.CompilerParams(vmem_limit_bytes=56 * 1024 * 1024),
        name="grid_columns",
    )(
        words, codes_all, jnp.asarray(bit_table()), s.reshape(1).astype(I32),
        x_all, taps, jnp.asarray(first), jnp.asarray(second), jnp.asarray(turn),
    )
    got = lax.all_to_all(sent, BOTH, split_axis=0, concat_axis=0, tiled=True)
    first, turn, last = row_tables()
    return pl.pallas_call(
        image_kernel,
        out_shape=jax.ShapeDtypeStruct((2, 64, GRID), F32),
        grid=(4,),
        in_specs=[
            pl.BlockSpec((DEVICES, 16, 128), lambda i: (0, i, 0)),
            pl.BlockSpec((256, 256), lambda i: (0, 0)),
            pl.BlockSpec((3, 256, 128), lambda i: (0, 0, 0)),
            pl.BlockSpec((64, 256), lambda i: (0, 0)),
        ],
        out_specs=pl.BlockSpec((2, 16, GRID), lambda i: (0, i, 0)),
        scratch_shapes=[
            pltpu.VMEM((DEVICES * 16, 128), F32),
            pltpu.VMEM((16 * 64, 128), F32),
            pltpu.VMEM((16 * 64, 128), F32),
        ],
        compiler_params=pltpu.CompilerParams(vmem_limit_bytes=48 * 1024 * 1024),
        name="image_rows",
    )(got, jnp.asarray(first), jnp.asarray(turn), jnp.asarray(last))


def solution(mesh):
    in_specs = (
        P(BOTH, None, None, None),
        P(BOTH, None),
        P(BOTH, None),
        P(BOTH, None),
        P(BOTH, None),
        P(BOTH),
        P(BOTH, None),
        P(),
    )
    out_specs = P(None, BOTH, None)
    return jax.shard_map(shards, mesh=mesh, in_specs=in_specs, out_specs=out_specs, check_vma=False)
```

time: 912 us -> 227 us (0.25); the launches traced: 899 us -> 226 us
  local copies, waits for them, and re-layouts: 374 us -> 3.11 us
  matrix products: 152 us -> 0 us
  other arithmetic: 139 us -> 4.47 us
  waiting for transfers between devices: 99.7 us -> 1.51 us
  Pallas kernels: 0 us -> 84.6 us
  starting transfers between devices: 29.3 us -> 0.01 us
  blocking collectives: 104 us -> 119 us
  between operations: 0.64 us -> 13.5 us
    dot_general x27 -> x0, matrix products: 152 us -> none  [the longest x4 43.3 us: make_patches(): jnp.einsum('bpckt,bkta->bpcka', weighted, row_hit, preferred_element_type...]
    all_to_all x3 -> x0, waiting for transfers between devices: 99.7 us -> none  [the longest x1 93.4 us: shards(): lax.all_to_all(stacked, 'vert', split_axis=1, concat_axis=2, tiled=True)]
    pallas_call x0 -> x3, Pallas kernels: none -> 84.6 us  [the longest x1 52.1 us: shards(): pl.pallas_call(grid_kernel, out_shape=jax.ShapeDtypeStruct((DEVICES, 64,...]
    another operation x12 -> x4, local copies, waits for them, and re-layouts: 72.7 us -> 0.06 us  [shards(): jnp.stack([row_offset, col_offset, kernel_index, jnp.zeros_like(row_offse...]
    unnamed x0 -> x1, blocking collectives: none -> 69.6 us
    scatter-add x3 -> x0, local copies, waits for them, and re-layouts: 64.6 us -> none  [the longest x1 45.8 us: shards(): extended = extended.at[:, :, :TILE_R, CELL:].add(right_part)]
    scatter-add x7 -> x0, other arithmetic: 64 us -> none  [the longest x4 38 us: grid_group(): return (cell_sums.at[cells_group].add(patches), None)]
    all_to_all x1, blocking collectives: 104 us -> 49.6 us  [shards(): got = lax.all_to_all(sent, BOTH, split_axis=0, concat_axis=0, tiled=True)]
  transfers between devices with their start and end apart: 5 -> 1, of which waited for: 3 -> 1; matrix products, arithmetic and copies ran while one was open for 3% -> 1% of each run, Pallas kernels for 0% -> 0%
where the time goes in v1:
time: 227 us; the launch traced here: 226 us
  blocking collectives  119 us (52%)
  Pallas kernels  84.6 us (37%)
  between operations  13.5 us (6%)
  other arithmetic  4.47 us (2%)
  local copies, waits for them, and re-layouts  3.11 us (1%)
    unnamed x1, blocking collectives  69.6 us
    pallas_call x1, Pallas kernels, shards(): pl.pallas_call(grid_kernel, out_shape=jax.ShapeDtypeStruct((DEVICES, 64,...  52.1 us
    all_to_all x1, blocking collectives, shards(): got = lax.all_to_all(sent, BOTH, split_axis=0, concat_axis=0, tiled=True)  49.6 us
    pallas_call x1, Pallas kernels, shards(): pl.pallas_call(image_kernel, out_shape=jax.ShapeDtypeStruct((2, 64, GRID)...  23.7 us
    pallas_call x1, Pallas kernels, shards(): pl.pallas_call(sort_kernel, out_shape=jax.ShapeDtypeStruct((NB_DEV * 16,...  8.82 us
  transfers between devices with their start and end apart: 1, of which 1 were waited for; matrix products, arithmetic and copies ran while one was open for 1% of the time, Pallas kernels for 0%

profile of v1, /device:TPU:1, one launch (start us, length us, event | category | flops | bytes accessed | tf_op | source)
XLA Modules:
  0.0 226.4 jit_solution(10547187084793746496)
XLA Ops:
  6.5 0.0 all-gather.2.cloned.1.call-start
  6.5 0.7 broadcast_compare_fusion
  7.3 0.7 convert_bitcast_fusion
  8.0 0.7 convert_bitcast_fusion.2
  8.7 0.7 convert_bitcast_fusion.1
  9.5 0.8 reshape.62
  10.3 0.7 concatenate.7.x_ref
  11.1 8.8 %sort_blocks.1 = bf16[256,128]{1,0:T(8,128)(2,1)} custom-call(bf16[16,8,256]{2,1,0:T(8,128)(2,1)} %concatenate.7.x_ref), custom_call_target="tpu_custom_call" | custom-call | tf_op jit(solution)/shard_map/sort_blocks/pallas_call | solution.py:365
  19.9 0.0 all-gather.2.cloned.1.call-update
  19.9 0.9 fusion.8
  20.8 0.1 copy.23
  20.9 0.1 copy.24
  21.0 0.8 fusion.6
  21.8 69.6 %all-reduce.meta = s32[2048]{0:T(1024)S(1)} all-reduce(s32[2048]{0:T(1024)S(1)} %fusion.6), channel_id=1, replica_groups=mesh['au'=16,'vert'=8] {'au','vert'}, use_global_device_ids=true, to_apply=%add | all-reduce | flops 2048 | bytes 16384
  91.3 0.0 copy-start.3
  91.4 0.1 reshape.88
  91.4 0.1 reshape.86
  91.5 0.1 reshape.90
  91.6 0.1 reshape.80
  91.7 0.1 reshape.84
  91.8 0.1 reshape.82
  91.9 0.2 or_reduce_fusion.2
  92.0 0.6 pad_add_fusion.words
  92.6 1.5 all-gather.2.cloned.1.call-done.x_ref
  94.1 0.0 copy-done.3
  94.1 52.1 %grid_columns.1 = bf16[128,64,128]{2,1,0:T(8,128)(2,1)} custom-call(s32[384]{0:T(512)} %pad_add_fusion.words, s32[2048]{0:T(1024)} %copy-done.3, s32[32]{0:T(128)} %constant.76.clone.bits, s32[1]{0:T(128)} %bitcast.7.strip, bf16[32768,128]{1,0:T(8,128)(2,1)} %all-gather.2.cloned.1.call-done.x_ref, f32[32,32]{1,0:T(8,128)} %bitcast.25, ...), custom_call_target="tpu_custom_call" | custom-call | tf_op jit(solution)/shard_map/grid_columns/pallas_call | solution.py:381
  146.2 0.0 copy-start
  146.2 49.6 %all_to_all.5.in_ref = bf16[128,64,128]{2,1,0:T(8,128)(2,1)S(1)} all-to-all(bf16[128,64,128]{2,1,0:T(8,128)(2,1)} %grid_columns.1), channel_id=1, replica_groups=mesh['au'=16,'vert'=8] {'au','vert'}, dimensions={0} | all-to-all | bytes 4194304 | tf_op jit(solution)/shard_map/all_to_all | solution.py:400
  195.8 0.0 copy-done
  195.8 0.0 copy-done.1
  195.8 0.0 copy-done.2
  195.8 23.7 %image_rows.1 = f32[2,64,8192]{2,1,0:T(8,128)} custom-call(bf16[128,64,128]{2,1,0:T(8,128)(2,1)S(1)} %all_to_all.5.in_ref, bf16[256,256]{1,0:T(8,128)(2,1)S(1)} %copy-done.1, f32[3,256,128]{2,1,0:T(8,128)S(1)} %copy-done, bf16[64,256]{1,0:T(8,128)(2,1)S(1)} %copy-done.2), custom_call_target="tpu_custom_call" | custom-call | tf_op jit(solution)/shard_map/image_rows/pallas_call | solution.py:402
  (11 shorter events, 0.1 us)
Async XLA Ops:
  6.5 87.6 %all-gather.2.cloned.1.call-start = ((), (), s32[]{:S(2)}) async-start(), calls=%async_computation.1 | async-start | bytes 8454144 | tf_op jit(solution)/shard_map/all_gather | solution.py:377
  91.3 2.8 %copy-start.3 = (s32[2048]{0:T(1024)}, s32[2048]{0:T(1024)S(1)}, u32[]{:S(2)}) copy-start(s32[2048]{0:T(1024)S(1)} %all-reduce.meta) | copy-start | bytes 24580
  146.2 49.6 %copy-start = (f32[3,256,128]{2,1,0:T(8,128)S(1)}, f32[3,256,128]{2,1,0:T(8,128)}, u32[]{:S(2)}) copy-start(f32[3,256,128]{2,1,0:T(8,128)} %constant.81.clone.turn_ref) | copy-start | bytes 1179652
  146.2 49.6 %copy-start.1 = (bf16[256,256]{1,0:T(8,128)(2,1)S(1)}, bf16[256,256]{1,0:T(8,128)(2,1)}, u32[]{:S(2)}) copy-start(bf16[256,256]{1,0:T(8,128)(2,1)} %constant.80.clone.first_ref) | copy-start | bytes 393220
  146.2 49.6 %copy-start.2 = (bf16[64,256]{1,0:T(8,128)(2,1)S(1)}, bf16[64,256]{1,0:T(8,128)(2,1)}, u32[]{:S(2)}) copy-start(bf16[64,256]{1,0:T(8,128)(2,1)} %constant.82.clone.last_ref) | copy-start | bytes 98308
Sparse Core Ops, SparseCore 0:
  20.1 74.0 all-gather.1

commit v2 on v1

--- a/solution.py
+++ b/solution.py
@@ -114,6 +114,104 @@
     lax.fori_loop(0, NB_DEV, one_block, 0, unroll=2)
 
 
+AGR = 272
+PARTS = ((0, 48, 48), (96, 48, 48), (192, 48, 32))
+ORDERS = (("x", "y", "z"), ("y", "z", "x"), ("z", "x", "y"))
+
+
+def gather_kernel(x_ref, meta_ref, all_ref, send, recv):
+    au, vert = lax.axis_index("au"), lax.axis_index("vert")
+    here = {"y": au // 4, "z": au % 4, "x": vert // 2}
+    core = vert % 2
+
+    def device(at, core):
+        return (at["y"] * 4 + at["z"], at["x"] * 2 + core)
+
+    def moved(dim, step):
+        return {**here, dim: (here[dim] + step) % 4}
+
+    sibling = device(here, 1 - core)
+    barrier = pltpu.get_barrier_semaphore()
+    for other in [device(moved(d, step), core) for d in "xyz" for step in (1, 3)] + [sibling]:
+        pl.semaphore_signal(barrier, inc=1, device_id=other, device_id_type=pl.DeviceIdType.MESH)
+    all_ref[here["y"], here["z"], here["x"], core, :256, :] = x_ref[...]
+    all_ref[here["y"], here["z"], here["x"], core, 256:, :] = meta_ref[...]
+    pl.semaphore_wait(barrier, 7)
+
+    def region(part, full, at, rows=None):
+        first, one, two = PARTS[part]
+        start, size = {None: (first, one + two), 0: (first, one), 1: (first + one, two)}[rows]
+        index = [slice(None) if d in full else at[d] for d in "yzx"]
+        return all_ref.at[(*index, core, pl.ds(start, size), slice(None))]
+
+    used = [0]
+    started = []
+
+    def copy(ref, to):
+        n = used[0]
+        used[0] += 1
+        made = pltpu.make_async_remote_copy(
+            src_ref=ref, dst_ref=ref, send_sem=send.at[n], recv_sem=recv.at[n],
+            device_id=to, device_id_type=pl.DeviceIdType.MESH,
+        )
+        made.start()
+        started.append(made)
+        return made
+
+    shared = []
+    for phase in range(3):
+        plain, relayed = [], []
+        for part, order in enumerate(ORDERS):
+            full, dim = order[:phase], order[phase]
+            ref = region(part, full, here)
+            right = copy(ref, device(moved(dim, 1), core))
+            left = copy(ref, device(moved(dim, 3), core))
+            plain.append((right, left))
+        if phase == 2:
+            for part, order in enumerate(ORDERS):
+                shared.append(copy(region(part, order[:2], here), sibling))
+        for part, order in enumerate(ORDERS):
+            full, dim = order[:phase], order[phase]
+            right, left = plain[part]
+            right.wait_recv()
+            one = copy(region(part, full, moved(dim, 3), 0), device(moved(dim, 1), core))
+            if phase == 2:
+                shared.append(copy(region(part, full, moved(dim, 3)), sibling))
+            left.wait_recv()
+            two = copy(region(part, full, moved(dim, 1), 1), device(moved(dim, 3), core))
+            if phase == 2:
+                shared.append(copy(region(part, full, moved(dim, 1)), sibling))
+            relayed.append((one, two))
+        for part, order in enumerate(ORDERS):
+            full, dim = order[:phase], order[phase]
+            for half, made in enumerate(relayed[part]):
+                made.wait_recv()
+                if phase == 2:
+                    shared.append(copy(region(part, full, moved(dim, 2), half), sibling))
+    for made in shared:
+        made.wait_recv()
+    for made in started:
+        made.wait_send()
+
+
+COPIES = 3 * (4 * 3 + 5)
+
+
+def gathered(ordered, meta):
+    vmem = pl.BlockSpec(memory_space=pltpu.VMEM)
+    return pl.pallas_call(
+        gather_kernel,
+        out_shape=jax.ShapeDtypeStruct((4, 4, 4, 2, AGR, 128), BF16),
+        in_specs=[vmem, vmem],
+        out_specs=vmem,
+        scratch_shapes=[pltpu.SemaphoreType.DMA((COPIES,)), pltpu.SemaphoreType.DMA((COPIES,))],
+        compiler_params=pltpu.CompilerParams(
+            collective_id=0, has_side_effects=True, vmem_limit_bytes=32 * 1024 * 1024
+        ),
+        name="gather_blocks",
+    )(ordered, meta)
+
+
 def pick(halves, index, low):
     first, second = [jnp.take_along_axis(half, index, axis=0, mode="promise_in_bounds") for half in halves]
     return jnp.where(low, first, second)
@@ -163,7 +261,7 @@
         cell = (where >> 14) & 31
         anchor_row = (where >> 19) * TILE_R + (cell >> 3) * 128
         anchor_col = ((block >> 4) & 7) * TILE_C + (cell & 7) * 128
-        x = x_ref[pl.ds(pl.multiple_of(block * 16, 16), 16), :].astype(F32)
+        x = x_ref[block >> 4, pl.ds(pl.multiple_of((block & 15) * 16, 16), 16), :].astype(F32)
         x = jnp.where(half == 1, x[8:], x[:8])
         row, col, wplane = [x[i : i + 1].astype(I32) for i in (4, 5, 6)]
         chosen = ones_where(iota((32, 128), 0) == wplane)
@@ -372,9 +470,11 @@
     by_block = ordered.reshape(NB_DEV, 16, 128)
     top = by_block[:, 4, 127].astype(I32)
     bottom = by_block[:, 12, 0].astype(I32)
-    code = ((tile_row[:, 0] * 32 + cell_index) << 14) | (top << 7) | bottom
-    codes_all = lax.all_gather(code, BOTH, axis=0, tiled=True)
-    x_all = lax.all_gather(ordered, BOTH, axis=0, tiled=True)
+    meta = jnp.stack([tile_row[:, 0].astype(BF16), cell_index.astype(BF16), by_block[:, 4, 127], by_block[:, 12, 0]])
+    x_all = gathered(ordered, jnp.pad(meta, ((0, 12), (0, 128 - NB_DEV)))).reshape(DEVICES, AGR, 128)
+    found = x_all[:, 256:260, :NB_DEV].astype(I32)
+    codes_all = ((found[:, 0] * 32 + found[:, 1]) << 14) | (found[:, 2] << 7) | found[:, 3]
+    codes_all = codes_all.reshape(BLOCKS)
     words = words_of(codes_all, s)
     first, second, turn = column_tables()
     taps = kernel_taps.transpose(1, 2, 0).reshape(2 * TAPS, 32)

time: 227 us -> 192 us (0.85)
  blocking collectives: 119 us -> 46 us
  Pallas kernels: 84.6 us -> 131 us
  between operations: 13.5 us -> 0.11 us
  local copies, waits for them, and re-layouts: 3.11 us -> 8.09 us
    unnamed x1 -> x0, blocking collectives: 69.6 us -> none
    pallas_call x0 -> x1, Pallas kernels: none -> 41.3 us  [gathered(): pl.pallas_call(gather_kernel, out_shape=jax.ShapeDtypeStruct((4, 4, 4, 2,...]
    pallas_call x1, Pallas kernels: 52.1 us -> 57.4 us  [shards(): pl.pallas_call(grid_kernel, out_shape=jax.ShapeDtypeStruct((DEVICES, 64,...]
    unnamed x11 -> x12, local copies, waits for them, and re-layouts: 0.2 us -> 4.45 us
    all_to_all x1, blocking collectives: 49.6 us -> 46 us  [shards(): got = lax.all_to_all(sent, BOTH, split_axis=0, concat_axis=0, tiled=True)]
  transfers between devices with their start and end apart: 1 -> 0, of which waited for: 1 -> 0; matrix products, arithmetic and copies ran while one was open for 1% -> 0% of each run, Pallas kernels for 0% -> 0%
where the time goes in v2:
time: 192 us
  Pallas kernels  131 us (68%)
  blocking collectives  46 us (24%)
  local copies, waits for them, and re-layouts  8.09 us (4%)
  other arithmetic  6.33 us (3%)
    pallas_call x1, Pallas kernels, shards(): pl.pallas_call(grid_kernel, out_shape=jax.ShapeDtypeStruct((DEVICES, 64,...  57.4 us
    all_to_all x1, blocking collectives, shards(): got = lax.all_to_all(sent, BOTH, split_axis=0, concat_axis=0, tiled=True)  46 us
    pallas_call x1, Pallas kernels, gathered(): pl.pallas_call(gather_kernel, out_shape=jax.ShapeDtypeStruct((4, 4, 4, 2,...  41.3 us
    pallas_call x1, Pallas kernels, shards(): pl.pallas_call(image_kernel, out_shape=jax.ShapeDtypeStruct((2, 64, GRID)...  23.7 us
    pallas_call x1, Pallas kernels, shards(): pl.pallas_call(sort_kernel, out_shape=jax.ShapeDtypeStruct((NB_DEV * 16,...  8.81 us
    unnamed x12, local copies, waits for them, and re-layouts  4.45 us

profile of v2, /device:TPU:1, one launch (start us, length us, event | category | flops | bytes accessed | tf_op | source)
XLA Modules:
  0.0 191.8 jit_solution(7474636609370116037)
XLA Ops:
  0.0 0.7 convert_bitcast_fusion.3
  0.7 0.7 convert_bitcast_fusion.4
  1.3 0.7 broadcast_compare_fusion
  2.0 0.7 convert_bitcast_fusion
  2.8 0.7 convert_bitcast_fusion.2
  3.5 0.7 convert_bitcast_fusion.1
  4.3 0.8 reshape.84
  5.1 0.7 concatenate.7.x_ref
  5.9 8.8 %sort_blocks.1.x_ref = bf16[256,128]{1,0:T(8,128)(2,1)} custom-call(bf16[16,8,256]{2,1,0:T(8,128)(2,1)} %concatenate.7.x_ref), custom_call_target="tpu_custom_call" | custom-call | tf_op jit(solution)/shard_map/sort_blocks/pallas_call | solution.py:463
  14.7 0.9 fusion.24
  15.5 0.1 copy.54
  15.6 0.1 copy.55
  15.7 0.0 copy-start.2
  15.8 0.8 copy-done.2
  16.6 41.3 %gather_blocks.1 = bf16[4,4,4,2,272,128]{5,4,3,2,1,0:T(8,128)(2,1)S(1)} custom-call(bf16[256,128]{1,0:T(8,128)(2,1)S(1)} %copy-done.2, bf16[16,128]{1,0:T(8,128)(2,1)S(1)} %fusion.19.meta_ref), custom_call_target="tpu_custom_call" | custom-call | tf_op jit(solution)/shard_map/gather_blocks/pallas_call | solution.py:202
  57.9 0.0 copy-start
  57.9 3.4 %copy-done = bf16[4,4,4,2,272,128]{5,4,3,2,1,0:T(8,128)(2,1)} copy-done((bf16[4,4,4,2,272,128]{5,4,3,2,1,0:T(8,128)(2,1)}, bf16[4,4,4,2,272,128]{5,4,3,2,1,0:T(8,128)(2,1)S(1)}, u32[]{:S(2)}) %copy-start) | copy-done | bytes 8912920
  61.3 0.1 slice_convert_fusion
  61.4 0.5 broadcast.272
  61.9 1.0 fusion.23
  63.0 0.7 reshape.90.meta
  63.6 0.2 fusion
  63.8 0.2 fusion.8
  64.0 0.6 pad_add_fusion.words
  64.6 57.4 %grid_columns.1 = bf16[128,64,128]{2,1,0:T(8,128)(2,1)} custom-call(s32[384]{0:T(512)} %pad_add_fusion.words, s32[2048]{0:T(1024)} %reshape.90.meta, s32[32]{0:T(128)} %constant.76.clone.bits, s32[1]{0:T(128)} %bitcast.19.strip, bf16[128,272,128]{2,1,0:T(8,128)(2,1)} %bitcast.50, f32[32,32]{1,0:T(8,128)} %bitcast.59, ...), custom_call_target="tpu_custom_call" | custom-call | tf_op jit(solution)/shard_map/grid_columns/pallas_call | solution.py:481
  122.0 0.0 copy-start.1
  122.0 0.0 copy-start.3
  122.0 46.0 %all_to_all.5.in_ref = bf16[128,64,128]{2,1,0:T(8,128)(2,1)S(1)} all-to-all(bf16[128,64,128]{2,1,0:T(8,128)(2,1)} %grid_columns.1), channel_id=1, replica_groups=mesh['au'=16,'vert'=8] {'au','vert'}, dimensions={0} | all-to-all | bytes 4194304 | tf_op jit(solution)/shard_map/all_to_all | solution.py:500
  168.1 0.0 copy-done.1
  168.1 0.0 copy-done.3
  168.1 0.0 copy-done.4
  168.1 23.7 %image_rows.1 = f32[2,64,8192]{2,1,0:T(8,128)} custom-call(bf16[128,64,128]{2,1,0:T(8,128)(2,1)S(1)} %all_to_all.5.in_ref, bf16[256,256]{1,0:T(8,128)(2,1)S(1)} %copy-done.3, f32[3,256,128]{2,1,0:T(8,128)S(1)} %copy-done.1, bf16[64,256]{1,0:T(8,128)(2,1)S(1)} %copy-done.4), custom_call_target="tpu_custom_call" | custom-call | tf_op jit(solution)/shard_map/image_rows/pallas_call | solution.py:502
  (12 shorter events, 0.2 us)
Async XLA Ops:
  15.7 0.8 copy-start.2
  57.9 3.4 %copy-start = (bf16[4,4,4,2,272,128]{5,4,3,2,1,0:T(8,128)(2,1)}, bf16[4,4,4,2,272,128]{5,4,3,2,1,0:T(8,128)(2,1)S(1)}, u32[]{:S(2)}) copy-start(bf16[4,4,4,2,272,128]{5,4,3,2,1,0:T(8,128)(2,1)S(1)} %gather_blocks.1) | copy-start | bytes 26738692
  122.0 46.0 %copy-start.1 = (f32[3,256,128]{2,1,0:T(8,128)S(1)}, f32[3,256,128]{2,1,0:T(8,128)}, u32[]{:S(2)}) copy-start(f32[3,256,128]{2,1,0:T(8,128)} %constant.81.clone.turn_ref) | copy-start | bytes 1179652
  122.0 46.0 %copy-start.3 = (bf16[256,256]{1,0:T(8,128)(2,1)S(1)}, bf16[256,256]{1,0:T(8,128)(2,1)}, u32[]{:S(2)}) copy-start(bf16[256,256]{1,0:T(8,128)(2,1)} %constant.80.clone.first_ref) | copy-start | bytes 393220
  122.0 46.0 %copy-start.4 = (bf16[64,256]{1,0:T(8,128)(2,1)S(1)}, bf16[64,256]{1,0:T(8,128)(2,1)}, u32[]{:S(2)}) copy-start(bf16[64,256]{1,0:T(8,128)(2,1)} %constant.82.clone.last_ref) | copy-start | bytes 98308

commit v3 on v2

--- a/solution.py
+++ b/solution.py
@@ -20,7 +20,8 @@
 ROWS = 32
 HEAD = 16
 WINDOW = 152
-UNROLL = 4
+UNROLL = 8
+BATCH = 32
 BOTH = ("au", "vert")
 F32 = jnp.float32
 BF16 = jnp.bfloat16
@@ -92,16 +93,26 @@
     return lax.dot_general(a, b, NT, preferred_element_type=F32)
 
 
-def sort_kernel(x_ref, out_ref):
+def sort_kernel(vis_ref, keep_ref, plane_ref, row_ref, col_ref, cell_ref, tile_ref, out_ref, meta):
     below = ones_where(iota((128, 128), 1) < iota((128, 128), 0))
     before = ones_where(iota((KVIS, KVIS), 0) < iota((KVIS, KVIS), 1))
     ones = jnp.ones((KVIS, KVIS), BF16)
     value = iota((128, KVIS), 0)
     place = iota((KVIS, KVIS), 0)
+    slot = iota((8, KVIS), 0)
+    lane = iota((1, 128), 1)
 
     def one_block(i, carry):
-        x = x_ref[i]
-        row = x.astype(F32)[4:5].astype(I32)
+        at = pl.ds(i, 1)
+        row = row_ref[at, :]
+        keep = keep_ref[at, :] == 1
+        x = jnp.where(slot == 4, row, jnp.where(slot == 5, col_ref[at, :], jnp.where(slot == 6, plane_ref[at, :], 0)))
+        x = x.astype(F32)
+        for p in range(2):
+            pair = vis_ref[i, p].astype(F32)
+            for c in range(2):
+                x = jnp.where((slot == 2 * p + c) & keep, pair[c : c + 1], x)
+        x = x.astype(BF16)
         hit = value == row
         hot = ones_where(hit)
         rank = dot(hot, before) + dot(dot(below, hot).astype(BF16), ones)
@@ -109,9 +120,13 @@
         moved = dot_nt(x, ones_where(place == rank.astype(I32)))
         both = jnp.concatenate([moved[:, :128], moved[:, 128:]], axis=0)
         out_ref[pl.ds(pl.multiple_of(i * 16, 16), 16), :] = both.astype(BF16)
+        note = jnp.where(lane == 0, tile_ref[i], jnp.where(lane == 1, cell_ref[i], 0)).astype(F32)
+        note = jnp.where(lane == 2, moved[4:5, 127:128], jnp.where(lane == 3, moved[4:5, 128:129], note))
+        meta[at, :] = note
         return carry
 
-    lax.fori_loop(0, NB_DEV, one_block, 0, unroll=2)
+    lax.fori_loop(0, NB_DEV, one_block, 0, unroll=4)
+    out_ref[256:, :] = meta[...].astype(BF16)
 
 
 AGR = 272
@@ -119,7 +134,7 @@
 ORDERS = (("x", "y", "z"), ("y", "z", "x"), ("z", "x", "y"))
 
 
-def gather_kernel(x_ref, meta_ref, all_ref, send, recv):
+def gather_kernel(x_ref, all_ref, send, recv, local):
     au, vert = lax.axis_index("au"), lax.axis_index("vert")
     here = {"y": au // 4, "z": au % 4, "x": vert // 2}
     core = vert % 2
@@ -132,11 +147,12 @@
 
     sibling = device(here, 1 - core)
     barrier = pltpu.get_barrier_semaphore()
-    for other in [device(moved(d, step), core) for d in "xyz" for step in (1, 3)] + [sibling]:
+    for other in [device(moved(d, step), core) for d in "xyz" for step in (1, 2, 3)] + [sibling]:
         pl.semaphore_signal(barrier, inc=1, device_id=other, device_id_type=pl.DeviceIdType.MESH)
-    all_ref[here["y"], here["z"], here["x"], core, :256, :] = x_ref[...]
-    all_ref[here["y"], here["z"], here["x"], core, 256:, :] = meta_ref[...]
-    pl.semaphore_wait(barrier, 7)
+    own = pltpu.make_async_copy(x_ref, all_ref.at[here["y"], here["z"], here["x"], core], local)
+    own.start()
+    own.wait()
+    pl.semaphore_wait(barrier, 10)
 
     def region(part, full, at, rows=None):
         first, one, two = PARTS[part]
@@ -159,7 +175,14 @@
         return made
 
     shared = []
-    for phase in range(3):
+    for phase in range(2):
+        direct = []
+        for part, order in enumerate(ORDERS):
+            ref = region(part, order[:phase], here)
+            direct += [copy(ref, device(moved(order[phase], step), core)) for step in (2, 1, 3)]
+        for made in direct:
+            made.wait_recv()
+    for phase in (2,):
         plain, relayed = [], []
         for part, order in enumerate(ORDERS):
             full, dim = order[:phase], order[phase]
@@ -194,22 +217,22 @@
         made.wait_send()
 
 
-COPIES = 3 * (4 * 3 + 5)
-
-
-def gathered(ordered, meta):
-    vmem = pl.BlockSpec(memory_space=pltpu.VMEM)
+COPIES = 3 * (3 + 3 + 4 + 5)
+
+
+def gathered(ordered):
+    anywhere = pl.BlockSpec(memory_space=pl.ANY)
     return pl.pallas_call(
         gather_kernel,
         out_shape=jax.ShapeDtypeStruct((4, 4, 4, 2, AGR, 128), BF16),
-        in_specs=[vmem, vmem],
-        out_specs=vmem,
-        scratch_shapes=[pltpu.SemaphoreType.DMA((COPIES,)), pltpu.SemaphoreType.DMA((COPIES,))],
-        compiler_params=pltpu.CompilerParams(
-            collective_id=0, has_side_effects=True, vmem_limit_bytes=32 * 1024 * 1024
-        ),
+        in_specs=[anywhere],
+        out_specs=anywhere,
+        scratch_shapes=[
+            pltpu.SemaphoreType.DMA((COPIES,)), pltpu.SemaphoreType.DMA((COPIES,)), pltpu.SemaphoreType.DMA
+        ],
+        compiler_params=pltpu.CompilerParams(collective_id=0, has_side_effects=True),
         name="gather_blocks",
-    )(ordered, meta)
+    )(ordered)
 
 
 def pick(halves, index, low):
@@ -231,10 +254,14 @@
 
 
 def grid_kernel(
-    words, meta, bits, strip, x_ref, taps_ref, first_ref, second_ref, turn_ref,
-    out_ref, acc, mid, stage, acc4, extra, items,
+    words, meta, bits, strip, x_all, first_all, taps_ref, second_ref, turn_ref,
+    out_ref, acc, mid, stage, acc4, extra, x_ref, first_ref, spread, items, sems,
 ):
     s = strip[0]
+    fetch_x = pltpu.make_async_copy(x_all, x_ref, sems.at[0])
+    fetch_x.start()
+    fetch_first = pltpu.make_async_copy(first_all, first_ref, sems.at[1])
+    fetch_first.start()
     acc[...] = jnp.zeros_like(acc)
     acc4[...] = jnp.zeros_like(acc4)
     table = taps_ref[...]
@@ -255,16 +282,20 @@
 
         return lax.fori_loop(0, 128, group, count)
 
-    def loaded(code):
-        half, block = code & 1, (code >> 1) & (BLOCKS - 1)
+    def place_of(code):
+        block = (code >> 1) & (BLOCKS - 1)
         where = meta[block]
         cell = (where >> 14) & 31
         anchor_row = (where >> 19) * TILE_R + (cell >> 3) * 128
-        anchor_col = ((block >> 4) & 7) * TILE_C + (cell & 7) * 128
+        return anchor_row, ((block >> 4) & 7) * TILE_C + (cell & 7) * 128
+
+    def codes_of(code):
+        half, block = code & 1, (code >> 1) & (BLOCKS - 1)
         x = x_ref[block >> 4, pl.ds(pl.multiple_of((block & 15) * 16, 16), 16), :].astype(F32)
-        x = jnp.where(half == 1, x[8:], x[:8])
-        row, col, wplane = [x[i : i + 1].astype(I32) for i in (4, 5, 6)]
-        chosen = ones_where(iota((32, 128), 0) == wplane)
+        return jnp.where(half == 1, x[8:], x[:8])
+
+    def factors_of(x):
+        chosen = ones_where(iota((32, 128), 0) == x[6:7].astype(I32))
         taps = dot(both_tables, chosen)
         tap_re, tap_im = taps[:16], taps[16:32]
         full_re, full_im = tap_re + taps[32:48], tap_im + taps[48:64]
@@ -273,11 +304,18 @@
             re, im = x[2 * p : 2 * p + 1], x[2 * p + 1 : 2 * p + 2]
             weights_re.append((re * full_re - im * full_im).astype(BF16).astype(F32))
             weights_im.append((re * full_im + im * full_re).astype(BF16).astype(F32))
-        limit = jnp.minimum(jnp.where(anchor_col == GRID - 128, 128, 1000) - col, TAPS)
-        return anchor_row, anchor_col, row, col, (tap_re, tap_im), weights_re + weights_im, limit
-
-    def item(code, valid):
-        anchor_row, anchor_col, row, col, taps, weights, limit = loaded(code)
+        return weights_re + weights_im + [tap_re, tap_im]
+
+    def offsets(x, anchor_col):
+        row, col = x[4:5].astype(I32), x[5:6].astype(I32)
+        return row, col, jnp.minimum(jnp.where(anchor_col == GRID - 128, 128, 1000) - col, TAPS)
+
+    def item(code, valid, slot):
+        anchor_row, anchor_col = place_of(code)
+        row, col, limit = offsets(codes_of(code), anchor_col)
+        base_at = pl.multiple_of(slot * 96, 96)
+        factors = [spread[pl.ds(base_at + 16 * i, 16), :] for i in range(6)]
+        weights, taps = factors[:4], factors[4:]
         mirror = (code >> 12) == 1
         sign = jnp.where(mirror, -1, 1)
         base = jnp.where(mirror, GRID - s * ROWS, s * ROWS) - anchor_row
@@ -297,24 +335,49 @@
         return pl.multiple_of(start, 16), patch
 
     count = listed(1, listed(0, 0))
-
-    def several(i, carry):
-        found = []
-        for k in range(UNROLL):
-            n = i * UNROLL + k
+    fetch_x.wait()
+
+    def batch(i, carry):
+        first_item = i * BATCH
+        rounds = (jnp.minimum(count - first_item, BATCH) + UNROLL - 1) // UNROLL
+
+        def code_at(n):
             valid = n < count
-            found.append(item(jnp.where(valid, items[n], 0), valid))
-        for start, patch in found:
-            acc[pl.ds(start, WINDOW), :] += patch
+            return jnp.where(valid, items[n], 0), valid
+
+        def prepare(r, carry):
+            for k in range(UNROLL):
+                slot = r * UNROLL + k
+                factors = factors_of(codes_of(code_at(first_item + slot)[0]))
+                for f, factor in enumerate(factors):
+                    spread[pl.ds(pl.multiple_of(slot * 96 + f * 16, 16), 16), :] = factor
+            return carry
+
+        lax.fori_loop(0, rounds, prepare, 0)
+
+        def several(r, carry):
+            found = []
+            for k in range(UNROLL):
+                slot = r * UNROLL + k
+                found.append(item(*code_at(first_item + slot), slot))
+            for start, patch in found:
+                acc[pl.ds(start, WINDOW), :] += patch
+            return carry
+
+        lax.fori_loop(0, rounds, several, 0)
         return carry
 
-    lax.fori_loop(0, (count + UNROLL - 1) // UNROLL, several, 0)
+    lax.fori_loop(0, (count + BATCH - 1) // BATCH, batch, 0)
     acc[HEAD : HEAD + 8, :] += jnp.where(iota((8, 128), 0) == 0, acc[HEAD + GRID : HEAD + GRID + 8, :], 0.0)
 
     count4 = listed(2, 0)
 
     def single(i, carry):
-        anchor_row, anchor_col, row, col, taps, weights, limit = loaded(items[i])
+        anchor_row, anchor_col = place_of(items[i])
+        x = codes_of(items[i])
+        row, col, limit = offsets(x, anchor_col)
+        factors = factors_of(x)
+        weights, taps = factors[:4], factors[4:]
         tap = jnp.broadcast_to(GRID // 2 - anchor_row - row, (8, 128))
         re0, re1, im0, im1 = placed(weights, tap, TAPS)
         q = iota((8, 128), 0)
@@ -335,9 +398,7 @@
     lane = iota((1, 128), 1)
     flip = jnp.where(lane < 64, -1.0, 1.0)
 
-    @pl.when(s != 0)
-    def _():
-        extra[...] = jnp.zeros_like(extra)
+    fetch_first.wait()
 
     @pl.when(s == 0)
     def _():
@@ -366,10 +427,9 @@
         mid[pl.ds(pl.multiple_of(c0 * 64, 64), 64), :] = y
         return carry
 
-    lax.fori_loop(0, 128, column_first, 0, unroll=4)
-
-    special = (s == 0) & ((lane == 64) | (lane == 96))
-    keep = jnp.where(special, 0.0, 1.0)
+    lax.fori_loop(0, 128, column_first, 0, unroll=16)
+
+    keep = jnp.where((lane == 64) | (lane == 96), 0.0, 1.0)
     second_hi = second_ref[:128]
     second_lo = second_ref[128:]
     spot = iota((64, 128), 0)
@@ -383,12 +443,22 @@
             turned = flip * pltpu.roll(y, 64, 1)
             pair = jnp.concatenate([y.astype(BF16), turned.astype(BF16)], axis=0)
             z = dot(second_hi, pair) + dot(second_lo, pair)
-            more = dot(extra[0], ones_where((spot == v0) & (spot_lane == 64)))
-            more = more + dot(extra[1], ones_where((spot == v0) & (spot_lane == 96)))
-            stage[pl.ds(v, 128, stride=16), :] = z * keep + more
+            stage[pl.ds(v, 128, stride=16), :] = z
             return carry
 
-        lax.fori_loop(0, 16, column_second, 0, unroll=2)
+        lax.fori_loop(0, 16, column_second, 0, unroll=8)
+
+        @pl.when(s == 0)
+        def _():
+            def middle(v, carry):
+                v0 = group * 16 + v
+                more = dot(extra[0], ones_where((spot == v0) & (spot_lane == 64)))
+                more = more + dot(extra[1], ones_where((spot == v0) & (spot_lane == 96)))
+                where = pl.ds(v, 128, stride=16)
+                stage[where, :] = stage[where, :] * keep + more
+                return carry
+
+            lax.fori_loop(0, 16, middle, 0, unroll=4)
 
         def pack(d, carry):
             out_ref[d, group * 16 : group * 16 + 16, :] = stage[
@@ -420,7 +490,7 @@
         right[pl.ds(pl.multiple_of(v * 64, 64), 64), :] = result[:, 128:]
         return carry
 
-    lax.fori_loop(0, 16, one, 0, unroll=2)
+    lax.fori_loop(0, 16, one, 0, unroll=8)
 
     def place(u1, carry):
         for p in range(2):
@@ -431,7 +501,7 @@
                     )
         return carry
 
-    lax.fori_loop(0, 32, place, 0, unroll=2)
+    lax.fori_loop(0, 32, place, 0, unroll=4)
 
 
 def words_of(code, s):
@@ -453,35 +523,14 @@
     return jnp.concatenate([packed(direct, direct + ROWS - 1), packed(mirror, mirror + ROWS - 1), middle])
 
 
-def shards(visibilities, keep_flags, kernel_index, row_offset, col_offset, cell_index, tile_row, kernel_taps):
-    s = lax.axis_index("au") * 8 + lax.axis_index("vert")
-    masked = jnp.where(keep_flags[:, None, :] == 1, visibilities.reshape(NB_DEV, 4, KVIS), 0).astype(BF16)
-    codes = jnp.stack([row_offset, col_offset, kernel_index, jnp.zeros_like(row_offset)], axis=1)
-    x8 = jnp.concatenate([masked, codes.astype(BF16)], axis=1)
+def gridded(words, codes_all, s, x_all, taps):
     vmem = pl.BlockSpec(memory_space=pltpu.VMEM)
     smem = pl.BlockSpec(memory_space=pltpu.SMEM)
-    ordered = pl.pallas_call(
-        sort_kernel,
-        out_shape=jax.ShapeDtypeStruct((NB_DEV * 16, 128), BF16),
-        in_specs=[vmem],
-        out_specs=vmem,
-        name="sort_blocks",
-    )(x8)
-    by_block = ordered.reshape(NB_DEV, 16, 128)
-    top = by_block[:, 4, 127].astype(I32)
-    bottom = by_block[:, 12, 0].astype(I32)
-    meta = jnp.stack([tile_row[:, 0].astype(BF16), cell_index.astype(BF16), by_block[:, 4, 127], by_block[:, 12, 0]])
-    x_all = gathered(ordered, jnp.pad(meta, ((0, 12), (0, 128 - NB_DEV)))).reshape(DEVICES, AGR, 128)
-    found = x_all[:, 256:260, :NB_DEV].astype(I32)
-    codes_all = ((found[:, 0] * 32 + found[:, 1]) << 14) | (found[:, 2] << 7) | found[:, 3]
-    codes_all = codes_all.reshape(BLOCKS)
-    words = words_of(codes_all, s)
     first, second, turn = column_tables()
-    taps = kernel_taps.transpose(1, 2, 0).reshape(2 * TAPS, 32)
-    sent = pl.pallas_call(
+    return pl.pallas_call(
         grid_kernel,
         out_shape=jax.ShapeDtypeStruct((DEVICES, 64, 128), BF16),
-        in_specs=[smem] * 4 + [vmem] * 5,
+        in_specs=[smem] * 4 + [pl.BlockSpec(memory_space=pl.ANY)] * 2 + [vmem] * 3,
         out_specs=vmem,
         scratch_shapes=[
             pltpu.VMEM((HEAD + GRID + 32, 128), F32),
@@ -489,15 +538,21 @@
             pltpu.VMEM((DEVICES * 16, 128), F32),
             pltpu.VMEM((66 * 8, 128), F32),
             pltpu.VMEM((2, 128, 64), BF16),
+            pltpu.VMEM((DEVICES, AGR, 128), BF16),
+            pltpu.VMEM((128, 128, 128), BF16),
+            pltpu.VMEM((BATCH * 96, 128), F32),
             pltpu.SMEM((4096,), I32),
+            pltpu.SemaphoreType.DMA((2,)),
         ],
-        compiler_params=pltpu.CompilerParams(vmem_limit_bytes=56 * 1024 * 1024),
+        compiler_params=pltpu.CompilerParams(vmem_limit_bytes=44 * 1024 * 1024),
         name="grid_columns",
     )(
         words, codes_all, jnp.asarray(bit_table()), s.reshape(1).astype(I32),
-        x_all, taps, jnp.asarray(first), jnp.asarray(second), jnp.asarray(turn),
+        x_all, jnp.asarray(first), taps, jnp.asarray(second), jnp.asarray(turn),
     )
-    got = lax.all_to_all(sent, BOTH, split_axis=0, concat_axis=0, tiled=True)
+
+
+def imaged(got):
     first, turn, last = row_tables()
     return pl.pallas_call(
         image_kernel,
@@ -520,6 +575,29 @@
     )(got, jnp.asarray(first), jnp.asarray(turn), jnp.asarray(last))
 
 
+def shards(visibilities, keep_flags, kernel_index, row_offset, col_offset, cell_index, tile_row, kernel_taps):
+    s = lax.axis_index("au") * 8 + lax.axis_index("vert")
+    vmem = pl.BlockSpec(memory_space=pltpu.VMEM)
+    smem = pl.BlockSpec(memory_space=pltpu.SMEM)
+    ordered = pl.pallas_call(
+        sort_kernel,
+        out_shape=jax.ShapeDtypeStruct((AGR, 128), BF16),
+        in_specs=[vmem] * 5 + [smem] * 2,
+        out_specs=vmem,
+        scratch_shapes=[pltpu.VMEM((16, 128), F32)],
+        name="sort_blocks",
+    )(visibilities, keep_flags, kernel_index, row_offset, col_offset, cell_index, tile_row.reshape(NB_DEV))
+    x_all = gathered(ordered).reshape(DEVICES, AGR, 128)
+    found = x_all[:, 256:, :4].astype(I32)
+    codes_all = ((found[..., 0] * 32 + found[..., 1]) << 14) | (found[..., 2] << 7) | found[..., 3]
+    codes_all = codes_all.reshape(BLOCKS)
+    words = words_of(codes_all, s)
+    taps = kernel_taps.transpose(1, 2, 0).reshape(2 * TAPS, 32)
+    sent = gridded(words, codes_all, s, x_all, taps)
+    got = lax.all_to_all(sent, BOTH, split_axis=0, concat_axis=0, tiled=True)
+    return imaged(got)
+
+
 def solution(mesh):
     in_specs = (
         P(BOTH, None, None, None),

time: 192 us -> 164 us (0.85)
  Pallas kernels: 131 us -> 97.8 us
  blocking collectives: 46 us -> 48.9 us
  other arithmetic: 6.33 us -> 8.53 us
    pallas_call x3, Pallas kernels: 89.9 us -> 58.6 us  [the longest x1 36.7 us: gridded(): pl.pallas_call(grid_kernel, out_shape=jax.ShapeDtypeStruct((DEVICES, 64,...]
    convert_element_type x0 -> x6, local copies, waits for them, and re-layouts: none -> 6.35 us  [the longest x3 3.73 us: packed(): two = (hit & (bottom <= final)).astype(I32)]
    convert_element_type x1, other arithmetic: 0.17 us -> 4.18 us  [packed(): one = (hit & (top >= first - (TAPS - 1))).astype(I32)]
    all_to_all x1, blocking collectives: 46 us -> 48.9 us  [shards(): got = lax.all_to_all(sent, BOTH, split_axis=0, concat_axis=0, tiled=True)]
    another operation x5 -> x0, other arithmetic: 2.84 us -> none  [the longest x3 2.17 us: shards(): jnp.stack([row_offset, col_offset, kernel_index, jnp.zeros_like(row_offse...]
    unnamed x12 -> x16, local copies, waits for them, and re-layouts: 4.45 us -> 2.22 us
    or x1, other arithmetic: 1 us -> 3.07 us  [shards(): found[..., 0] * 32 + found[..., 1] << 14 | found[..., 2] << 7]
    pallas_call x1, Pallas kernels: 41.3 us -> 39.3 us  [gathered(): pl.pallas_call(gather_kernel, out_shape=jax.ShapeDtypeStruct((4, 4, 4, 2,...]
where the time goes in v3:
time: 164 us
  Pallas kernels  97.8 us (60%)
  blocking collectives  48.9 us (30%)
  local copies, waits for them, and re-layouts  8.65 us (5%)
  other arithmetic  8.53 us (5%)
    all_to_all x1, blocking collectives, shards(): got = lax.all_to_all(sent, BOTH, split_axis=0, concat_axis=0, tiled=True)  48.9 us
    pallas_call x1, Pallas kernels, gathered(): pl.pallas_call(gather_kernel, out_shape=jax.ShapeDtypeStruct((4, 4, 4, 2,...  39.3 us
    pallas_call x1, Pallas kernels, gridded(): pl.pallas_call(grid_kernel, out_shape=jax.ShapeDtypeStruct((DEVICES, 64,...  36.7 us
    pallas_call x1, Pallas kernels, imaged(): pl.pallas_call(image_kernel, out_shape=jax.ShapeDtypeStruct((2, 64, GRID)...  13.7 us
    pallas_call x1, Pallas kernels, shards(): pl.pallas_call(sort_kernel, out_shape=jax.ShapeDtypeStruct((AGR, 128), BF...  8.13 us
    convert_element_type x1, other arithmetic, packed(): one = (hit & (top >= first - (TAPS - 1))).astype(I32)  4.18 us
    convert_element_type x3, local copies, waits for them, and re-layouts, packed(): two = (hit & (bottom <= final)).astype(I32)  3.73 us

profile of v3, /device:TPU:1, one launch (start us, length us, event | category | flops | bytes accessed | tf_op | source)
XLA Modules:
  0.0 164.1 jit_solution(2025586928127696365)
XLA Ops:
  0.0 8.1 %sort_blocks.1.x_ref = bf16[272,128]{1,0:T(8,128)(2,1)} custom-call(bf16[16,2,2,256]{3,2,1,0:T(2,128)(2,1)} %vis_ref.1, s32[16,256]{1,0:T(8,128)} %keep_ref.1, s32[16,256]{1,0:T(8,128)} %plane_ref.1, s32[16,256]{1,0:T(8,128)} %row_ref.1, s32[16,256]{1,0:T(8,128)} %col_ref.1, s32[16]{0:T(128)} %cell_ref.1, s32[16]{0:T(128)} %bitcast.39), custom_call_target="tpu_custom_call" | custom-call | tf_op jit(solution)/shard_map/sort_blocks/pallas_call | solution.py:582
  8.1 39.3 %gather_blocks.1 = bf16[4,4,4,2,272,128]{5,4,3,2,1,0:T(8,128)(2,1)} custom-call(bf16[272,128]{1,0:T(8,128)(2,1)} %sort_blocks.1.x_ref), custom_call_target="tpu_custom_call" | custom-call | tf_op jit(solution)/shard_map/gather_blocks/pallas_call | solution.py:225
  47.4 1.2 slice_convert_fusion
  48.6 3.1 %fusion.14 = (s32[128,16]{1,0:T(8,128)S(1)}, s32[128,16,1]{2,1,0:T(8,128)}) fusion(s32[128,16,4]{2,1,0:T(8,128)S(1)} %slice_convert_fusion), kind=kLoop, calls=%fused_computation.39 | loop fusion | flops 12288 | bytes 49152 | tf_op jit(solution)/shard_map/or | solution.py:592
  51.6 0.1 reshape.73.meta
  51.7 4.2 %fusion.3 = (s32[128,16,1]{2,1,0:T(8,128)}, s32[128,16,1]{2,1,0:T(8,128)}, s32[128,16,1]{2,1,0:T(8,128)}, s32[128,16,1]{2,1,0:T(8,128)S(1)}, s32[128,16,1]{2,1,0:T(8,128)S(1)}, /*index=5*/s32[128,16,1]{2,1,0:T(8,128)S(1)}) fusion(s32[128,16,1]{2,1,0:T(8,128)} %get-tuple-element.9, s32[]{:T(128)S(6)} %mul.53, s32[]{:T(128)S(6)} %sub.51), kind=kLoop, calls=%fused_computation.12 | loop fusion | flops 90112 | bytes 57352 | tf_op jit(solution)/shard_map/convert_element_type | solution.py:514
  55.9 0.0 copy-start.2
  55.9 0.0 copy-start.4
  55.9 0.0 copy-start.6
  55.9 0.0 copy-start.7
  55.9 1.7 %copy.119 = s32[128,16,1]{0,1,2:T(8,128)S(1)} copy(s32[128,16,1]{2,1,0:T(8,128)} %get-tuple-element.10) | data formatting | bytes 16384 | tf_op jit(solution)/shard_map/convert_element_type | solution.py:514
  57.6 1.6 copy.116
  59.2 1.6 copy.118
  60.9 0.5 copy.115
  61.3 0.5 copy.117
  61.8 0.5 copy.120
  62.3 0.1 fusion.13
  62.4 0.0 copy-done.2
  62.4 0.0 copy-done.4
  62.4 0.0 copy-done.6
  62.4 0.0 copy-done.7
  62.4 0.0 copy-start
  62.4 2.2 %copy-done = bf16[128,128,128]{2,1,0:T(8,128)(2,1)S(1)} copy-done((bf16[128,128,128]{2,1,0:T(8,128)(2,1)S(1)}, bf16[128,128,128]{2,1,0:T(8,128)(2,1)}, u32[]{:S(2)}) %copy-start) | copy-done | bytes 4194328
  64.6 36.7 %grid_columns.1 = bf16[128,64,128]{2,1,0:T(8,128)(2,1)S(1)} custom-call(s32[384]{0:T(512)S(1)} %pad_add_fusion.words, s32[2048]{0:T(1024)S(1)} %reshape.73.meta, s32[32]{0:T(128)S(1)} %copy-done.7, s32[1]{0:T(128)} %bitcast.8.strip, bf16[128,272,128]{2,1,0:T(8,128)(2,1)} %bitcast.38, bf16[128,128,128]{2,1,0:T(8,128)(2,1)S(1)} %copy-done, ...), custom_call_target="tpu_custom_call" | custom-call | tf_op jit(solution)/shard_map/grid_columns/pallas_call | solution.py:530
  101.3 0.0 copy-start.1
  101.4 0.0 copy-start.3
  101.4 0.0 copy-start.5
  101.4 48.9 %all_to_all.5.in_ref = bf16[128,64,128]{2,1,0:T(8,128)(2,1)S(1)} all-to-all(bf16[128,64,128]{2,1,0:T(8,128)(2,1)S(1)} %grid_columns.1), channel_id=1, replica_groups=mesh['au'=16,'vert'=8] {'au','vert'}, dimensions={0} | all-to-all | bytes 4194304 | tf_op jit(solution)/shard_map/all_to_all | solution.py:597
  150.3 0.0 copy-done.1
  150.3 0.0 copy-done.3
  150.3 0.0 copy-done.5
  150.3 13.7 %image_rows.1 = f32[2,64,8192]{2,1,0:T(8,128)} custom-call(bf16[128,64,128]{2,1,0:T(8,128)(2,1)S(1)} %all_to_all.5.in_ref, bf16[256,256]{1,0:T(8,128)(2,1)S(1)} %copy-done.3, f32[3,256,128]{2,1,0:T(8,128)S(1)} %copy-done.1, bf16[64,256]{1,0:T(8,128)(2,1)S(1)} %copy-done.5), custom_call_target="tpu_custom_call" | custom-call | tf_op jit(solution)/shard_map/image_rows/pallas_call | solution.py:557
  (3 shorter events, 0.0 us)
Async XLA Ops:
  55.9 6.5 %copy-start.2 = (bf16[256,256]{1,0:T(8,128)(2,1)S(1)}, bf16[256,256]{1,0:T(8,128)(2,1)}, u32[]{:S(2)}) copy-start(bf16[256,256]{1,0:T(8,128)(2,1)} %constant.72.clone.second_ref) | copy-start | bytes 393220
  55.9 6.5 %copy-start.4 = (f32[128,128]{1,0:T(8,128)S(1)}, f32[128,128]{1,0:T(8,128)}, u32[]{:S(2)}) copy-start(f32[128,128]{1,0:T(8,128)} %constant.73.clone.turn_ref) | copy-start | bytes 196612
  55.9 6.5 %copy-start.6 = (f32[32,2,16]{0,2,1:T(8,128)S(1)}, f32[32,2,16]{0,2,1:T(8,128)}, u32[]{:S(2)}) copy-start(f32[32,2,16]{0,2,1:T(8,128)} %param.22) | copy-start | bytes 12292
  55.9 6.5 %copy-start.7 = (s32[32]{0:T(128)S(1)}, s32[32]{0:T(128)}, u32[]{:S(2)}) copy-start(s32[32]{0:T(128)} %constant.70.clone.bits) | copy-start | bytes 388
  62.4 2.2 %copy-start = (bf16[128,128,128]{2,1,0:T(8,128)(2,1)S(1)}, bf16[128,128,128]{2,1,0:T(8,128)(2,1)}, u32[]{:S(2)}) copy-start(bf16[128,128,128]{2,1,0:T(8,128)(2,1)} %constant.71.clone.first_all) | copy-start | bytes 12582916
  101.3 49.0 %copy-start.1 = (f32[3,256,128]{2,1,0:T(8,128)S(1)}, f32[3,256,128]{2,1,0:T(8,128)}, u32[]{:S(2)}) copy-start(f32[3,256,128]{2,1,0:T(8,128)} %constant.75.clone.turn_ref) | copy-start | bytes 1179652
  101.4 49.0 %copy-start.3 = (bf16[256,256]{1,0:T(8,128)(2,1)S(1)}, bf16[256,256]{1,0:T(8,128)(2,1)}, u32[]{:S(2)}) copy-start(bf16[256,256]{1,0:T(8,128)(2,1)} %constant.74.clone.first_ref) | copy-start | bytes 393220
  101.4 49.0 %copy-start.5 = (bf16[64,256]{1,0:T(8,128)(2,1)S(1)}, bf16[64,256]{1,0:T(8,128)(2,1)}, u32[]{:S(2)}) copy-start(bf16[64,256]{1,0:T(8,128)(2,1)} %constant.76.clone.last_ref) | copy-start | bytes 98308

commit v4 on v3

--- a/solution.py
+++ b/solution.py
@@ -101,6 +101,8 @@
     place = iota((KVIS, KVIS), 0)
     slot = iota((8, KVIS), 0)
     lane = iota((1, 128), 1)
+
+    meta[...] = jnp.zeros_like(meta)
 
     def one_block(i, carry):
         at = pl.ds(i, 1)
@@ -126,7 +128,8 @@
         return carry
 
     lax.fori_loop(0, NB_DEV, one_block, 0, unroll=4)
-    out_ref[256:, :] = meta[...].astype(BF16)
+    turned = dot_nt(ones_where(iota((16, 128), 0) == iota((16, 128), 1)), meta[...].astype(BF16))
+    out_ref[256:, :] = turned.astype(BF16)
 
 
 AGR = 272
@@ -269,7 +272,7 @@
     table_lo = (table - table_hi.astype(F32)).astype(BF16)
     both_tables = jnp.concatenate([table_hi, table_lo], axis=0)
 
-    def listed(kind, count):
+    def listed(kind, count, groups=128):
         def group(g, n):
             def step(state):
                 word, n = state
@@ -280,7 +283,7 @@
 
             return lax.while_loop(lambda state: state[0] != 0, step, (words[kind * 128 + g], n))[1]
 
-        return lax.fori_loop(0, 128, group, count)
+        return lax.fori_loop(0, groups, group, count)
 
     def place_of(code):
         block = (code >> 1) & (BLOCKS - 1)
@@ -370,7 +373,7 @@
     lax.fori_loop(0, (count + BATCH - 1) // BATCH, batch, 0)
     acc[HEAD : HEAD + 8, :] += jnp.where(iota((8, 128), 0) == 0, acc[HEAD + GRID : HEAD + GRID + 8, :], 0.0)
 
-    count4 = listed(2, 0)
+    count4 = listed(2, 0, jnp.where(s == 0, 128, 0))
 
     def single(i, carry):
         anchor_row, anchor_col = place_of(items[i])
@@ -584,12 +587,12 @@
         out_shape=jax.ShapeDtypeStruct((AGR, 128), BF16),
         in_specs=[vmem] * 5 + [smem] * 2,
         out_specs=vmem,
-        scratch_shapes=[pltpu.VMEM((16, 128), F32)],
+        scratch_shapes=[pltpu.VMEM((128, 128), F32)],
         name="sort_blocks",
     )(visibilities, keep_flags, kernel_index, row_offset, col_offset, cell_index, tile_row.reshape(NB_DEV))
     x_all = gathered(ordered).reshape(DEVICES, AGR, 128)
-    found = x_all[:, 256:, :4].astype(I32)
-    codes_all = ((found[..., 0] * 32 + found[..., 1]) << 14) | (found[..., 2] << 7) | found[..., 3]
+    found = x_all[:, 256:260, :NB_DEV].astype(I32)
+    codes_all = ((found[:, 0] * 32 + found[:, 1]) << 14) | (found[:, 2] << 7) | found[:, 3]
     codes_all = codes_all.reshape(BLOCKS)
     words = words_of(codes_all, s)
     taps = kernel_taps.transpose(1, 2, 0).reshape(2 * TAPS, 32)

time: 164 us -> 152 us (0.927)
  Pallas kernels: 97.8 us -> 90.3 us
  blocking collectives: 48.9 us -> 56.4 us
  other arithmetic: 8.53 us -> 2.47 us
  local copies, waits for them, and re-layouts: 8.65 us -> 2.82 us
    pallas_call x1, Pallas kernels: 36.7 us -> 28.8 us  [gridded(): pl.pallas_call(grid_kernel, out_shape=jax.ShapeDtypeStruct((DEVICES, 64,...]
    all_to_all x1, blocking collectives: 48.9 us -> 56.4 us  [shards(): got = lax.all_to_all(sent, BOTH, split_axis=0, concat_axis=0, tiled=True)]
    convert_element_type x6 -> x0, local copies, waits for them, and re-layouts: 6.35 us -> none  [the longest x3 3.73 us: packed(): two = (hit & (bottom <= final)).astype(I32)]
    convert_element_type x1, other arithmetic: 4.18 us -> 0.17 us  [packed(): one = (hit & (top >= first - (TAPS - 1))).astype(I32)]
    or x1, other arithmetic: 3.07 us -> 1.01 us  [shards(): found[:, 0] * 32 + found[:, 1] << 14 | found[:, 2] << 7 | found[:, 3]]
where the time goes in v4:
time: 152 us
  Pallas kernels  90.3 us (59%)
  blocking collectives  56.4 us (37%)
  local copies, waits for them, and re-layouts  2.82 us (2%)
  other arithmetic  2.47 us (2%)
    all_to_all x1, blocking collectives, shards(): got = lax.all_to_all(sent, BOTH, split_axis=0, concat_axis=0, tiled=True)  56.4 us
    pallas_call x1, Pallas kernels, gathered(): pl.pallas_call(gather_kernel, out_shape=jax.ShapeDtypeStruct((4, 4, 4, 2,...  39.5 us
    pallas_call x1, Pallas kernels, gridded(): pl.pallas_call(grid_kernel, out_shape=jax.ShapeDtypeStruct((DEVICES, 64,...  28.8 us
    pallas_call x1, Pallas kernels, imaged(): pl.pallas_call(image_kernel, out_shape=jax.ShapeDtypeStruct((2, 64, GRID)...  13.7 us
    pallas_call x1, Pallas kernels, shards(): pl.pallas_call(sort_kernel, out_shape=jax.ShapeDtypeStruct((AGR, 128), BF...  8.28 us

profile of v4, /device:TPU:1, one launch (start us, length us, event | category | flops | bytes accessed | tf_op | source)
XLA Modules:
  0.0 152.1 jit_solution(14459823174391385846)
XLA Ops:
  0.0 8.3 %sort_blocks.1.x_ref = bf16[272,128]{1,0:T(8,128)(2,1)} custom-call(bf16[16,2,2,256]{3,2,1,0:T(2,128)(2,1)} %vis_ref.1, s32[16,256]{1,0:T(8,128)} %keep_ref.1, s32[16,256]{1,0:T(8,128)} %plane_ref.1, s32[16,256]{1,0:T(8,128)} %row_ref.1, s32[16,256]{1,0:T(8,128)} %col_ref.1, s32[16]{0:T(128)} %cell_ref.1, s32[16]{0:T(128)} %bitcast.47), custom_call_target="tpu_custom_call" | custom-call | tf_op jit(solution)/shard_map/sort_blocks/pallas_call | solution.py:585
  8.3 0.0 copy-start.2
  8.3 0.0 copy-start.4
  8.3 0.0 copy-start.6
  8.3 0.0 copy-start.7
  8.3 39.5 %gather_blocks.1 = bf16[4,4,4,2,272,128]{5,4,3,2,1,0:T(8,128)(2,1)} custom-call(bf16[272,128]{1,0:T(8,128)(2,1)} %sort_blocks.1.x_ref), custom_call_target="tpu_custom_call" | custom-call | tf_op jit(solution)/shard_map/gather_blocks/pallas_call | solution.py:228
  47.8 1.0 slice_convert_fusion
  48.8 0.5 broadcast.247
  49.3 1.0 fusion.11
  50.4 0.1 reshape.73.meta
  50.5 0.2 fusion
  50.7 0.2 fusion.8
  50.9 0.0 copy-done.2
  50.9 0.0 copy-done.4
  50.9 0.0 copy-done.6
  50.9 0.0 copy-done.7
  50.9 0.0 copy-start
  50.9 2.2 %copy-done = bf16[128,128,128]{2,1,0:T(8,128)(2,1)S(1)} copy-done((bf16[128,128,128]{2,1,0:T(8,128)(2,1)S(1)}, bf16[128,128,128]{2,1,0:T(8,128)(2,1)}, u32[]{:S(2)}) %copy-start) | copy-done | bytes 4194328
  53.1 28.8 %grid_columns.1 = bf16[128,64,128]{2,1,0:T(8,128)(2,1)S(1)} custom-call(s32[384]{0:T(512)S(1)} %pad_add_fusion.words, s32[2048]{0:T(1024)S(1)} %reshape.73.meta, s32[32]{0:T(128)S(1)} %copy-done.7, s32[1]{0:T(128)} %bitcast.12.strip, bf16[128,272,128]{2,1,0:T(8,128)(2,1)} %bitcast.39, bf16[128,128,128]{2,1,0:T(8,128)(2,1)S(1)} %copy-done, ...), custom_call_target="tpu_custom_call" | custom-call | tf_op jit(solution)/shard_map/grid_columns/pallas_call | solution.py:533
  81.9 0.0 copy-start.1
  82.0 0.0 copy-start.3
  82.0 0.0 copy-start.5
  82.0 56.4 %all_to_all.5.in_ref = bf16[128,64,128]{2,1,0:T(8,128)(2,1)S(1)} all-to-all(bf16[128,64,128]{2,1,0:T(8,128)(2,1)S(1)} %grid_columns.1), channel_id=1, replica_groups=mesh['au'=16,'vert'=8] {'au','vert'}, dimensions={0} | all-to-all | bytes 4194304 | tf_op jit(solution)/shard_map/all_to_all | solution.py:600
  138.4 0.0 copy-done.1
  138.4 0.0 copy-done.3
  138.4 0.0 copy-done.5
  138.4 13.7 %image_rows.1 = f32[2,64,8192]{2,1,0:T(8,128)} custom-call(bf16[128,64,128]{2,1,0:T(8,128)(2,1)S(1)} %all_to_all.5.in_ref, bf16[256,256]{1,0:T(8,128)(2,1)S(1)} %copy-done.3, f32[3,256,128]{2,1,0:T(8,128)S(1)} %copy-done.1, bf16[64,256]{1,0:T(8,128)(2,1)S(1)} %copy-done.5), custom_call_target="tpu_custom_call" | custom-call | tf_op jit(solution)/shard_map/image_rows/pallas_call | solution.py:560
  (6 shorter events, 0.1 us)
Async XLA Ops:
  8.3 42.6 %copy-start.2 = (bf16[256,256]{1,0:T(8,128)(2,1)S(1)}, bf16[256,256]{1,0:T(8,128)(2,1)}, u32[]{:S(2)}) copy-start(bf16[256,256]{1,0:T(8,128)(2,1)} %constant.72.clone.second_ref) | copy-start | bytes 393220
  8.3 42.6 %copy-start.4 = (f32[128,128]{1,0:T(8,128)S(1)}, f32[128,128]{1,0:T(8,128)}, u32[]{:S(2)}) copy-start(f32[128,128]{1,0:T(8,128)} %constant.73.clone.turn_ref) | copy-start | bytes 196612
  8.3 42.6 %copy-start.6 = (f32[32,2,16]{0,2,1:T(8,128)S(1)}, f32[32,2,16]{0,2,1:T(8,128)}, u32[]{:S(2)}) copy-start(f32[32,2,16]{0,2,1:T(8,128)} %param.22) | copy-start | bytes 12292
  8.3 42.6 %copy-start.7 = (s32[32]{0:T(128)S(1)}, s32[32]{0:T(128)}, u32[]{:S(2)}) copy-start(s32[32]{0:T(128)} %constant.70.clone.bits) | copy-start | bytes 388
  50.9 2.2 %copy-start = (bf16[128,128,128]{2,1,0:T(8,128)(2,1)S(1)}, bf16[128,128,128]{2,1,0:T(8,128)(2,1)}, u32[]{:S(2)}) copy-start(bf16[128,128,128]{2,1,0:T(8,128)(2,1)} %constant.71.clone.first_all) | copy-start | bytes 12582916
  81.9 56.4 %copy-start.1 = (f32[3,256,128]{2,1,0:T(8,128)S(1)}, f32[3,256,128]{2,1,0:T(8,128)}, u32[]{:S(2)}) copy-start(f32[3,256,128]{2,1,0:T(8,128)} %constant.75.clone.turn_ref) | copy-start | bytes 1179652
  82.0 56.4 %copy-start.3 = (bf16[256,256]{1,0:T(8,128)(2,1)S(1)}, bf16[256,256]{1,0:T(8,128)(2,1)}, u32[]{:S(2)}) copy-start(bf16[256,256]{1,0:T(8,128)(2,1)} %constant.74.clone.first_ref) | copy-start | bytes 393220
  82.0 56.4 %copy-start.5 = (bf16[64,256]{1,0:T(8,128)(2,1)S(1)}, bf16[64,256]{1,0:T(8,128)(2,1)}, u32[]{:S(2)}) copy-start(bf16[64,256]{1,0:T(8,128)(2,1)} %constant.76.clone.last_ref) | copy-start | bytes 98308

commit v5 on v4

--- a/solution.py
+++ b/solution.py
@@ -20,8 +20,8 @@
 ROWS = 32
 HEAD = 16
 WINDOW = 152
-UNROLL = 8
-BATCH = 32
+UNROLL = 12
+BATCH = 48
 BOTH = ("au", "vert")
 F32 = jnp.float32
 BF16 = jnp.bfloat16
@@ -93,7 +93,7 @@
     return lax.dot_general(a, b, NT, preferred_element_type=F32)
 
 
-def sort_kernel(vis_ref, keep_ref, plane_ref, row_ref, col_ref, cell_ref, tile_ref, out_ref, meta):
+def sort_kernel(vis_ref, keep_ref, plane_ref, row_ref, col_ref, cell_ref, tile_ref, out_ref, meta, wide):
     below = ones_where(iota((128, 128), 1) < iota((128, 128), 0))
     before = ones_where(iota((KVIS, KVIS), 0) < iota((KVIS, KVIS), 1))
     ones = jnp.ones((KVIS, KVIS), BF16)
@@ -108,7 +108,10 @@
         at = pl.ds(i, 1)
         row = row_ref[at, :]
         keep = keep_ref[at, :] == 1
-        x = jnp.where(slot == 4, row, jnp.where(slot == 5, col_ref[at, :], jnp.where(slot == 6, plane_ref[at, :], 0)))
+        wplane = plane_ref[at, :]
+        first = (128 + row) << (wplane >> 2)
+        second = (128 + col_ref[at, :]) << (wplane & 3)
+        x = jnp.where(slot == 4, first, jnp.where(slot == 5, second, jnp.where(slot == 6, row, 0)))
         x = x.astype(F32)
         for p in range(2):
             pair = vis_ref[i, p].astype(F32)
@@ -120,20 +123,25 @@
         rank = dot(hot, before) + dot(dot(below, hot).astype(BF16), ones)
         rank = jnp.sum(jnp.where(hit, rank, 0.0), axis=0, keepdims=True)
         moved = dot_nt(x, ones_where(place == rank.astype(I32)))
-        both = jnp.concatenate([moved[:, :128], moved[:, 128:]], axis=0)
-        out_ref[pl.ds(pl.multiple_of(i * 16, 16), 16), :] = both.astype(BF16)
+        left, right = moved[:, :128], moved[:, 128:]
+        wide[pl.ds(pl.multiple_of(i * 8, 8), 8), :] = jnp.where(iota((8, 128), 0) < 4, left, pltpu.roll(right, 4, 0))
+        for k, part in enumerate((left[4:5], left[5:6], right[4:5], right[5:6])):
+            wide[pl.ds(CODES + i * 4 + k, 1), :] = part
         note = jnp.where(lane == 0, tile_ref[i], jnp.where(lane == 1, cell_ref[i], 0)).astype(F32)
-        note = jnp.where(lane == 2, moved[4:5, 127:128], jnp.where(lane == 3, moved[4:5, 128:129], note))
+        note = jnp.where(lane == 2, moved[6:7, 127:128], jnp.where(lane == 3, moved[6:7, 128:129], note))
         meta[at, :] = note
         return carry
 
-    lax.fori_loop(0, NB_DEV, one_block, 0, unroll=4)
+    lax.fori_loop(0, NB_DEV, one_block, 0, unroll=8)
     turned = dot_nt(ones_where(iota((16, 128), 0) == iota((16, 128), 1)), meta[...].astype(BF16))
-    out_ref[256:, :] = turned.astype(BF16)
-
-
-AGR = 272
-PARTS = ((0, 48, 48), (96, 48, 48), (192, 48, 32))
+    out_ref[:NOTES, :] = wide[...].astype(BF16)
+    out_ref[NOTES:, :] = turned.astype(BF16)
+
+
+AGR = 208
+CODES = 128
+NOTES = 192
+PARTS = ((0, 32, 32), (64, 32, 32), (128, 48, 32))
 ORDERS = (("x", "y", "z"), ("y", "z", "x"), ("z", "x", "y"))
 
 
@@ -265,8 +273,12 @@
     fetch_x.start()
     fetch_first = pltpu.make_async_copy(first_all, first_ref, sems.at[1])
     fetch_first.start()
-    acc[...] = jnp.zeros_like(acc)
-    acc4[...] = jnp.zeros_like(acc4)
+    acc[0] = jnp.zeros(acc.shape[1:], F32)
+
+    @pl.when(s == 0)
+    def _():
+        acc[1] = jnp.zeros(acc.shape[1:], F32)
+
     table = taps_ref[...]
     table_hi = table.astype(BF16)
     table_lo = (table - table_hi.astype(F32)).astype(BF16)
@@ -292,13 +304,23 @@
         anchor_row = (where >> 19) * TILE_R + (cell >> 3) * 128
         return anchor_row, ((block >> 4) & 7) * TILE_C + (cell & 7) * 128
 
-    def codes_of(code):
+    def values_of(code):
         half, block = code & 1, (code >> 1) & (BLOCKS - 1)
-        x = x_ref[block >> 4, pl.ds(pl.multiple_of((block & 15) * 16, 16), 16), :].astype(F32)
-        return jnp.where(half == 1, x[8:], x[:8])
-
-    def factors_of(x):
-        chosen = ones_where(iota((32, 128), 0) == x[6:7].astype(I32))
+        owner, own = block >> 4, block & 15
+        x = x_ref[owner, pl.ds(pl.multiple_of((own >> 1) * 16, 16), 16), :].astype(F32)
+        x = jnp.where((own & 1) == 1, x[8:], x[:8])
+        x = jnp.where(half == 1, pltpu.roll(x, 4, 0), x)
+        packed = x_ref[owner, pl.ds(pl.multiple_of(CODES + (own >> 2) * 16, 16), 16), :].astype(F32)
+        packed = jnp.where((own & 2) == 2, packed[8:], packed[:8])
+        packed = jnp.where((own & 1) == 1, pltpu.roll(packed, 4, 0), packed)
+        packed = jnp.where(half == 1, pltpu.roll(packed, 6, 0), packed).astype(I32)
+        first, second = packed[:1], packed[1:2]
+        power = sum([(first >= (128 << n)).astype(I32) for n in range(1, 8)])
+        power2 = sum([(second >= (128 << n)).astype(I32) for n in range(1, 4)])
+        return x, (first >> power) - 128, (second >> power2) - 128, power * 4 + power2
+
+    def factors_of(x, wplane):
+        chosen = ones_where(iota((32, 128), 0) == wplane)
         taps = dot(both_tables, chosen)
         tap_re, tap_im = taps[:16], taps[16:32]
         full_re, full_im = tap_re + taps[32:48], tap_im + taps[48:64]
@@ -309,23 +331,26 @@
             weights_im.append((re * full_im + im * full_re).astype(BF16).astype(F32))
         return weights_re + weights_im + [tap_re, tap_im]
 
-    def offsets(x, anchor_col):
-        row, col = x[4:5].astype(I32), x[5:6].astype(I32)
-        return row, col, jnp.minimum(jnp.where(anchor_col == GRID - 128, 128, 1000) - col, TAPS)
+    def limit_of(col, anchor_col):
+        return jnp.minimum(jnp.where(anchor_col == GRID - 128, 128, 1000) - col, TAPS)
 
     def item(code, valid, slot):
         anchor_row, anchor_col = place_of(code)
-        row, col, limit = offsets(codes_of(code), anchor_col)
-        base_at = pl.multiple_of(slot * 96, 96)
+        base_at = pl.multiple_of(slot * 104, 8)
+        where = spread[pl.ds(base_at + 96, 8), :].astype(I32)
+        row, col = where[:1], where[1:2]
+        limit = limit_of(col, anchor_col)
         factors = [spread[pl.ds(base_at + 16 * i, 16), :] for i in range(6)]
         weights, taps = factors[:4], factors[4:]
-        mirror = (code >> 12) == 1
+        kind = code >> 12
+        mirror, middle = kind == 1, kind == 2
         sign = jnp.where(mirror, -1, 1)
-        base = jnp.where(mirror, GRID - s * ROWS, s * ROWS) - anchor_row
+        base = jnp.where(middle, GRID // 2, jnp.where(mirror, GRID - s * ROWS, s * ROWS)) - anchor_row
         base = jnp.where(valid, base, -100000)
         least = jnp.where(mirror & (s == 0), 1, 0)
         j = iota((ROWS, 128), 0)
-        tap = jnp.where(j < least, -1, base + sign * j - row)
+        most = jnp.where(middle, 0, ROWS)
+        tap = jnp.where((j < least) | (j > most), -1, base + sign * j - row)
         re0, re1, im0, im1 = placed(weights, tap, TAPS)
         flip = jnp.where(mirror, -1.0, 1.0)
         left = jnp.concatenate([re0, re1, im0 * flip, im1 * flip], axis=0).astype(BF16)
@@ -335,9 +360,9 @@
         cols = jnp.concatenate([col_re.astype(BF16), col_im.astype(BF16)], axis=1)
         patch = dot_nt(cols, jnp.concatenate([left, right], axis=1))
         start = jnp.where(mirror, GRID - 128 - anchor_col, anchor_col + HEAD)
-        return pl.multiple_of(start, 16), patch
-
-    count = listed(1, listed(0, 0))
+        return middle.astype(I32), pl.multiple_of(start, 16), patch
+
+    count = listed(2, listed(1, listed(0, 0)), jnp.where(s == 0, 128, 0))
     fetch_x.wait()
 
     def batch(i, carry):
@@ -351,9 +376,11 @@
         def prepare(r, carry):
             for k in range(UNROLL):
                 slot = r * UNROLL + k
-                factors = factors_of(codes_of(code_at(first_item + slot)[0]))
-                for f, factor in enumerate(factors):
-                    spread[pl.ds(pl.multiple_of(slot * 96 + f * 16, 16), 16), :] = factor
+                x, row, col, wplane = values_of(code_at(first_item + slot)[0])
+                base_at = pl.multiple_of(slot * 104, 8)
+                for f, factor in enumerate(factors_of(x, wplane)):
+                    spread[pl.ds(base_at + f * 16, 16), :] = factor
+                spread[pl.ds(base_at + 96, 8), :] = jnp.where(iota((8, 128), 0) == 0, row, col).astype(F32)
             return carry
 
         lax.fori_loop(0, rounds, prepare, 0)
@@ -363,40 +390,15 @@
             for k in range(UNROLL):
                 slot = r * UNROLL + k
                 found.append(item(*code_at(first_item + slot), slot))
-            for start, patch in found:
-                acc[pl.ds(start, WINDOW), :] += patch
+            for target, start, patch in found:
+                acc[target, pl.ds(start, WINDOW), :] += patch
             return carry
 
         lax.fori_loop(0, rounds, several, 0)
         return carry
 
     lax.fori_loop(0, (count + BATCH - 1) // BATCH, batch, 0)
-    acc[HEAD : HEAD + 8, :] += jnp.where(iota((8, 128), 0) == 0, acc[HEAD + GRID : HEAD + GRID + 8, :], 0.0)
-
-    count4 = listed(2, 0, jnp.where(s == 0, 128, 0))
-
-    def single(i, carry):
-        anchor_row, anchor_col = place_of(items[i])
-        x = codes_of(items[i])
-        row, col, limit = offsets(x, anchor_col)
-        factors = factors_of(x)
-        weights, taps = factors[:4], factors[4:]
-        tap = jnp.broadcast_to(GRID // 2 - anchor_row - row, (8, 128))
-        re0, re1, im0, im1 = placed(weights, tap, TAPS)
-        q = iota((8, 128), 0)
-        left = jnp.where(q == 0, re0, jnp.where(q == 1, re1, jnp.where(q == 2, im0, jnp.where(q == 3, im1, 0.0))))
-        right = jnp.where(q == 0, -im0, jnp.where(q == 1, -im1, jnp.where(q == 2, re0, jnp.where(q == 3, re1, 0.0))))
-        rows = jnp.concatenate([left, right], axis=1).astype(BF16)
-        tap = iota((WINDOW, 128), 0) - col
-        col_re, col_im = placed(taps, tap, limit)
-        cols = jnp.concatenate([col_re, col_im], axis=1)
-        tail = jnp.concatenate([cols[128:], jnp.zeros((256 - WINDOW, 256), F32)], axis=0)
-        c1 = anchor_col >> 7
-        acc4[pl.ds(pl.multiple_of(c1 * 8, 8), 8), :] += dot_nt(rows, cols[:128].astype(BF16))
-        acc4[pl.ds(pl.multiple_of(c1 * 8 + 8, 8), 8), :] += dot_nt(rows, tail.astype(BF16))
-        return carry
-
-    lax.fori_loop(0, count4, single, 0)
+    acc[0, HEAD : HEAD + 8, :] += jnp.where(iota((8, 128), 0) == 0, acc[0, HEAD + GRID : HEAD + GRID + 8, :], 0.0)
 
     lane = iota((1, 128), 1)
     flip = jnp.where(lane < 64, -1.0, 1.0)
@@ -405,6 +407,14 @@
 
     @pl.when(s == 0)
     def _():
+        picked = ones_where(iota((8, 128), 1) == 32 * iota((8, 128), 0))
+
+        def turn_block(c1, carry):
+            block = acc[1, pl.ds(pl.multiple_of(HEAD + c1 * 128, 16), 128), :].astype(BF16)
+            acc4[pl.ds(pl.multiple_of(c1 * 8, 8), 8), :] = dot_nt(picked, block)
+            return carry
+
+        lax.fori_loop(0, 64, turn_block, 0, unroll=8)
         cosine = first_ref[0, :64, :64]
         sine = first_ref[0, 64:, :64]
         turn_cos, turn_sin = turn_ref[:64], turn_ref[64:]
@@ -415,11 +425,10 @@
             mid_im = dot(cosine, im) + dot(sine, re)
             turned_re = (mid_re * turn_cos - mid_im * turn_sin).astype(BF16)
             turned_im = (mid_re * turn_sin + mid_im * turn_cos).astype(BF16)
-            got = dot_nt(second_ref[:128, :128], turned_re) - dot_nt(second_ref[:128, 128:], turned_im)
-            extra[p] = got.astype(BF16)
+            extra[p] = dot(turned_re, second_ref[:128, :128]) - dot(turned_im, second_ref[:128, 128:])
 
     def column_first(c0, carry):
-        h = acc[pl.ds(HEAD + c0, 64, stride=128), :]
+        h = acc[0, pl.ds(HEAD + c0, 64, stride=128), :]
         high = h.astype(BF16)
         low = (h - high.astype(F32)).astype(BF16)
         factors = first_ref[c0]
@@ -432,11 +441,8 @@
 
     lax.fori_loop(0, 128, column_first, 0, unroll=16)
 
-    keep = jnp.where((lane == 64) | (lane == 96), 0.0, 1.0)
     second_hi = second_ref[:128]
     second_lo = second_ref[128:]
-    spot = iota((64, 128), 0)
-    spot_lane = iota((64, 128), 1)
 
     for group in range(4):
 
@@ -449,19 +455,7 @@
             stage[pl.ds(v, 128, stride=16), :] = z
             return carry
 
-        lax.fori_loop(0, 16, column_second, 0, unroll=8)
-
-        @pl.when(s == 0)
-        def _():
-            def middle(v, carry):
-                v0 = group * 16 + v
-                more = dot(extra[0], ones_where((spot == v0) & (spot_lane == 64)))
-                more = more + dot(extra[1], ones_where((spot == v0) & (spot_lane == 96)))
-                where = pl.ds(v, 128, stride=16)
-                stage[where, :] = stage[where, :] * keep + more
-                return carry
-
-            lax.fori_loop(0, 16, middle, 0, unroll=4)
+        lax.fori_loop(0, 16, column_second, 0, unroll=16)
 
         def pack(d, carry):
             out_ref[d, group * 16 : group * 16 + 16, :] = stage[
@@ -469,7 +463,24 @@
             ].astype(BF16)
             return carry
 
-        lax.fori_loop(0, 128, pack, 0, unroll=8)
+        def pack_middle(d, carry):
+            z = stage[pl.ds(pl.multiple_of(d * 16, 16), 16), :]
+            at = jnp.full((16, 128), d, I32)
+            for p in range(2):
+                middle = jnp.take_along_axis(
+                    extra[p, group * 16 : group * 16 + 16, :], at, axis=1, mode="promise_in_bounds"
+                )
+                z = jnp.where(lane == 64 + 32 * p, middle, z)
+            out_ref[d, group * 16 : group * 16 + 16, :] = z.astype(BF16)
+            return carry
+
+        @pl.when(s != 0)
+        def _():
+            lax.fori_loop(0, 128, pack, 0, unroll=8)
+
+        @pl.when(s == 0)
+        def _():
+            lax.fori_loop(0, 128, pack_middle, 0, unroll=8)
 
 
 def image_kernel(in_ref, first_ref, turn_ref, last_ref, out_ref, wide, left, right):
@@ -493,7 +504,7 @@
         right[pl.ds(pl.multiple_of(v * 64, 64), 64), :] = result[:, 128:]
         return carry
 
-    lax.fori_loop(0, 16, one, 0, unroll=8)
+    lax.fori_loop(0, 16, one, 0, unroll=16)
 
     def place(u1, carry):
         for p in range(2):
@@ -536,18 +547,18 @@
         in_specs=[smem] * 4 + [pl.BlockSpec(memory_space=pl.ANY)] * 2 + [vmem] * 3,
         out_specs=vmem,
         scratch_shapes=[
-            pltpu.VMEM((HEAD + GRID + 32, 128), F32),
+            pltpu.VMEM((2, HEAD + GRID + 32, 128), F32),
             pltpu.VMEM((128 * 64, 128), F32),
             pltpu.VMEM((DEVICES * 16, 128), F32),
-            pltpu.VMEM((66 * 8, 128), F32),
-            pltpu.VMEM((2, 128, 64), BF16),
+            pltpu.VMEM((64 * 8, 128), F32),
+            pltpu.VMEM((2, 64, 128), F32),
             pltpu.VMEM((DEVICES, AGR, 128), BF16),
             pltpu.VMEM((128, 128, 128), BF16),
-            pltpu.VMEM((BATCH * 96, 128), F32),
+            pltpu.VMEM((BATCH * 104, 128), F32),
             pltpu.SMEM((4096,), I32),
             pltpu.SemaphoreType.DMA((2,)),
         ],
-        compiler_params=pltpu.CompilerParams(vmem_limit_bytes=44 * 1024 * 1024),
+        compiler_params=pltpu.CompilerParams(vmem_limit_bytes=60 * 1024 * 1024),
         name="grid_columns",
     )(
         words, codes_all, jnp.asarray(bit_table()), s.reshape(1).astype(I32),
@@ -578,20 +589,26 @@
     )(got, jnp.asarray(first), jnp.asarray(turn), jnp.asarray(last))
 
 
-def shards(visibilities, keep_flags, kernel_index, row_offset, col_offset, cell_index, tile_row, kernel_taps):
-    s = lax.axis_index("au") * 8 + lax.axis_index("vert")
+def sorted_blocks(visibilities, keep_flags, kernel_index, row_offset, col_offset, cell_index, tile_row):
     vmem = pl.BlockSpec(memory_space=pltpu.VMEM)
     smem = pl.BlockSpec(memory_space=pltpu.SMEM)
-    ordered = pl.pallas_call(
+    return pl.pallas_call(
         sort_kernel,
         out_shape=jax.ShapeDtypeStruct((AGR, 128), BF16),
         in_specs=[vmem] * 5 + [smem] * 2,
         out_specs=vmem,
-        scratch_shapes=[pltpu.VMEM((128, 128), F32)],
+        scratch_shapes=[pltpu.VMEM((128, 128), F32), pltpu.VMEM((NOTES, 128), F32)],
         name="sort_blocks",
-    )(visibilities, keep_flags, kernel_index, row_offset, col_offset, cell_index, tile_row.reshape(NB_DEV))
+    )(visibilities, keep_flags, kernel_index, row_offset, col_offset, cell_index, tile_row)
+
+
+def shards(visibilities, keep_flags, kernel_index, row_offset, col_offset, cell_index, tile_row, kernel_taps):
+    s = lax.axis_index("au") * 8 + lax.axis_index("vert")
+    ordered = sorted_blocks(
+        visibilities, keep_flags, kernel_index, row_offset, col_offset, cell_index, tile_row.reshape(NB_DEV)
+    )
     x_all = gathered(ordered).reshape(DEVICES, AGR, 128)
-    found = x_all[:, 256:260, :NB_DEV].astype(I32)
+    found = x_all[:, NOTES : NOTES + 4, :NB_DEV].astype(I32)
     codes_all = ((found[:, 0] * 32 + found[:, 1]) << 14) | (found[:, 2] << 7) | found[:, 3]
     codes_all = codes_all.reshape(BLOCKS)
     words = words_of(codes_all, s)

time: 152 us -> 137 us (0.901)
  Pallas kernels: 90.3 us -> 79.8 us
  blocking collectives: 56.4 us -> 52.6 us
  local copies, waits for them, and re-layouts: 2.82 us -> 1.21 us
    pallas_call x1, Pallas kernels: 39.5 us -> 33.4 us  [gathered(): pl.pallas_call(gather_kernel, out_shape=jax.ShapeDtypeStruct((4, 4, 4, 2,...]
    all_to_all x1, blocking collectives: 56.4 us -> 52.6 us  [shards(): got = lax.all_to_all(sent, BOTH, split_axis=0, concat_axis=0, tiled=True)]
    unnamed x16 -> x6, local copies, waits for them, and re-layouts: 2.22 us -> 0.02 us
    pallas_call x1, Pallas kernels: 28.8 us -> 26.8 us  [gridded(): pl.pallas_call(grid_kernel, out_shape=jax.ShapeDtypeStruct((DEVICES, 64,...]
    pallas_call x1, Pallas kernels: 13.7 us -> 11.9 us  [imaged(): pl.pallas_call(image_kernel, out_shape=jax.ShapeDtypeStruct((2, 64, GRID)...]
where the time goes in v5:
time: 137 us
  Pallas kernels  79.8 us (58%)
  blocking collectives  52.6 us (38%)
  other arithmetic  3.05 us (2%)
    all_to_all x1, blocking collectives, shards(): got = lax.all_to_all(sent, BOTH, split_axis=0, concat_axis=0, tiled=True)  52.6 us
    pallas_call x1, Pallas kernels, gathered(): pl.pallas_call(gather_kernel, out_shape=jax.ShapeDtypeStruct((4, 4, 4, 2,...  33.4 us
    pallas_call x1, Pallas kernels, gridded(): pl.pallas_call(grid_kernel, out_shape=jax.ShapeDtypeStruct((DEVICES, 64,...  26.8 us
    pallas_call x1, Pallas kernels, imaged(): pl.pallas_call(image_kernel, out_shape=jax.ShapeDtypeStruct((2, 64, GRID)...  11.9 us
    pallas_call x1, Pallas kernels, sorted_blocks(): pl.pallas_call(sort_kernel, out_shape=jax.ShapeDtypeStruct((AGR, 128), BF...  7.69 us

profile of v5, /device:TPU:1, one launch (start us, length us, event | category | flops | bytes accessed | tf_op | source)
XLA Modules:
  0.0 136.8 jit_solution(1073036739397568562)
XLA Ops:
  0.0 7.7 %sort_blocks.1.x_ref = bf16[208,128]{1,0:T(8,128)(2,1)} custom-call(bf16[16,2,2,256]{3,2,1,0:T(2,128)(2,1)} %vis_ref.1, s32[16,256]{1,0:T(8,128)} %keep_ref.1, s32[16,256]{1,0:T(8,128)} %plane_ref.1, s32[16,256]{1,0:T(8,128)} %row_ref.1, s32[16,256]{1,0:T(8,128)} %col_ref.1, s32[16]{0:T(128)} %cell_ref.1, s32[16]{0:T(128)} %bitcast.47), custom_call_target="tpu_custom_call" | custom-call | tf_op jit(solution)/shard_map/sort_blocks/pallas_call | solution.py:595
  7.7 33.4 %gather_blocks.1 = bf16[4,4,4,2,208,128]{5,4,3,2,1,0:T(8,128)(2,1)} custom-call(bf16[208,128]{1,0:T(8,128)(2,1)} %sort_blocks.1.x_ref), custom_call_target="tpu_custom_call" | custom-call | tf_op jit(solution)/shard_map/gather_blocks/pallas_call | solution.py:236
  41.1 1.0 slice_convert_fusion
  42.2 0.5 broadcast.247
  42.7 1.0 fusion.11
  43.8 0.7 reshape.73.meta
  44.4 0.2 fusion
  44.6 0.2 fusion.8
  44.8 0.6 pad_add_fusion.words
  45.4 26.8 %grid_columns.1 = bf16[128,64,128]{2,1,0:T(8,128)(2,1)} custom-call(s32[384]{0:T(512)} %pad_add_fusion.words, s32[2048]{0:T(1024)} %reshape.73.meta, s32[32]{0:T(128)} %constant.70.clone.bits, s32[1]{0:T(128)} %bitcast.12.strip, bf16[128,208,128]{2,1,0:T(8,128)(2,1)} %bitcast.38, bf16[128,128,128]{2,1,0:T(8,128)(2,1)} %constant.71.clone.first_all, ...), custom_call_target="tpu_custom_call" | custom-call | tf_op jit(solution)/shard_map/grid_columns/pallas_call | solution.py:544
  72.2 0.0 copy-start
  72.2 0.0 copy-start.1
  72.2 0.0 copy-start.2
  72.2 52.6 %all_to_all.5.in_ref = bf16[128,64,128]{2,1,0:T(8,128)(2,1)S(1)} all-to-all(bf16[128,64,128]{2,1,0:T(8,128)(2,1)} %grid_columns.1), channel_id=1, replica_groups=mesh['au'=16,'vert'=8] {'au','vert'}, dimensions={0} | all-to-all | bytes 4194304 | tf_op jit(solution)/shard_map/all_to_all | solution.py:617
  124.9 0.0 copy-done
  124.9 0.0 copy-done.1
  124.9 0.0 copy-done.2
  124.9 11.9 %image_rows.1 = f32[2,64,8192]{2,1,0:T(8,128)} custom-call(bf16[128,64,128]{2,1,0:T(8,128)(2,1)S(1)} %all_to_all.5.in_ref, bf16[256,256]{1,0:T(8,128)(2,1)S(1)} %copy-done.1, f32[3,256,128]{2,1,0:T(8,128)S(1)} %copy-done, bf16[64,256]{1,0:T(8,128)(2,1)S(1)} %copy-done.2), custom_call_target="tpu_custom_call" | custom-call | tf_op jit(solution)/shard_map/image_rows/pallas_call | solution.py:571
  (5 shorter events, 0.1 us)
Async XLA Ops:
  72.2 52.7 %copy-start = (f32[3,256,128]{2,1,0:T(8,128)S(1)}, f32[3,256,128]{2,1,0:T(8,128)}, u32[]{:S(2)}) copy-start(f32[3,256,128]{2,1,0:T(8,128)} %constant.75.clone.turn_ref) | copy-start | bytes 1179652
  72.2 52.7 %copy-start.1 = (bf16[256,256]{1,0:T(8,128)(2,1)S(1)}, bf16[256,256]{1,0:T(8,128)(2,1)}, u32[]{:S(2)}) copy-start(bf16[256,256]{1,0:T(8,128)(2,1)} %constant.74.clone.first_ref) | copy-start | bytes 393220
  72.2 52.7 %copy-start.2 = (bf16[64,256]{1,0:T(8,128)(2,1)S(1)}, bf16[64,256]{1,0:T(8,128)(2,1)}, u32[]{:S(2)}) copy-start(bf16[64,256]{1,0:T(8,128)(2,1)} %constant.76.clone.last_ref) | copy-start | bytes 98308

commit v6 on v5

--- a/solution.py
+++ b/solution.py
@@ -20,8 +20,8 @@
 ROWS = 32
 HEAD = 16
 WINDOW = 152
-UNROLL = 12
-BATCH = 48
+UNROLL = 16
+BATCH = 64
 BOTH = ("au", "vert")
 F32 = jnp.float32
 BF16 = jnp.bfloat16
@@ -265,14 +265,14 @@
 
 
 def grid_kernel(
-    words, meta, bits, strip, x_all, first_all, taps_ref, second_ref, turn_ref,
+    words0, words1, words2, meta, bits, strip, x_all, first_all, taps_ref, second_ref, turn_ref,
     out_ref, acc, mid, stage, acc4, extra, x_ref, first_ref, spread, items, sems,
 ):
+    words = (words0, words1, words2)
     s = strip[0]
     fetch_x = pltpu.make_async_copy(x_all, x_ref, sems.at[0])
     fetch_x.start()
     fetch_first = pltpu.make_async_copy(first_all, first_ref, sems.at[1])
-    fetch_first.start()
     acc[0] = jnp.zeros(acc.shape[1:], F32)
 
     @pl.when(s == 0)
@@ -293,7 +293,7 @@
                 items[n] = (kind << 12) | ((g * NB_DEV + (bit & 15)) << 1) | (bit >> 4)
                 return word ^ low, n + 1
 
-            return lax.while_loop(lambda state: state[0] != 0, step, (words[kind * 128 + g], n))[1]
+            return lax.while_loop(lambda state: state[0] != 0, step, (words[kind][g], n))[1]
 
         return lax.fori_loop(0, groups, group, count)
 
@@ -319,7 +319,7 @@
         power2 = sum([(second >= (128 << n)).astype(I32) for n in range(1, 4)])
         return x, (first >> power) - 128, (second >> power2) - 128, power * 4 + power2
 
-    def factors_of(x, wplane):
+    def factors_of(x, wplane, flip):
         chosen = ones_where(iota((32, 128), 0) == wplane)
         taps = dot(both_tables, chosen)
         tap_re, tap_im = taps[:16], taps[16:32]
@@ -329,7 +329,7 @@
             re, im = x[2 * p : 2 * p + 1], x[2 * p + 1 : 2 * p + 2]
             weights_re.append((re * full_re - im * full_im).astype(BF16).astype(F32))
             weights_im.append((re * full_im + im * full_re).astype(BF16).astype(F32))
-        return weights_re + weights_im + [tap_re, tap_im]
+        return weights_re + [im * flip for im in weights_im] + [tap_re, tap_im * flip]
 
     def limit_of(col, anchor_col):
         return jnp.minimum(jnp.where(anchor_col == GRID - 128, 128, 1000) - col, TAPS)
@@ -352,9 +352,8 @@
         most = jnp.where(middle, 0, ROWS)
         tap = jnp.where((j < least) | (j > most), -1, base + sign * j - row)
         re0, re1, im0, im1 = placed(weights, tap, TAPS)
-        flip = jnp.where(mirror, -1.0, 1.0)
-        left = jnp.concatenate([re0, re1, im0 * flip, im1 * flip], axis=0).astype(BF16)
-        right = jnp.concatenate([-im0, -im1, re0 * flip, re1 * flip], axis=0).astype(BF16)
+        left = jnp.concatenate([re0, re1, im0, im1], axis=0).astype(BF16)
+        right = jnp.concatenate([-im0, -im1, re0, re1], axis=0).astype(BF16)
         tap = jnp.where(mirror, 144, 0) + sign * iota((WINDOW, 128), 0) - col
         col_re, col_im = placed(taps, tap, limit)
         cols = jnp.concatenate([col_re.astype(BF16), col_im.astype(BF16)], axis=1)
@@ -364,6 +363,7 @@
 
     count = listed(2, listed(1, listed(0, 0)), jnp.where(s == 0, 128, 0))
     fetch_x.wait()
+    fetch_first.start()
 
     def batch(i, carry):
         first_item = i * BATCH
@@ -376,9 +376,11 @@
         def prepare(r, carry):
             for k in range(UNROLL):
                 slot = r * UNROLL + k
-                x, row, col, wplane = values_of(code_at(first_item + slot)[0])
+                code = code_at(first_item + slot)[0]
+                x, row, col, wplane = values_of(code)
+                flip = jnp.where((code >> 12) == 1, -1.0, 1.0)
                 base_at = pl.multiple_of(slot * 104, 8)
-                for f, factor in enumerate(factors_of(x, wplane)):
+                for f, factor in enumerate(factors_of(x, wplane, flip)):
                     spread[pl.ds(base_at + f * 16, 16), :] = factor
                 spread[pl.ds(base_at + 96, 8), :] = jnp.where(iota((8, 128), 0) == 0, row, col).astype(F32)
             return carry
@@ -441,6 +443,7 @@
 
     lax.fori_loop(0, 128, column_first, 0, unroll=16)
 
+    spots = ones_where(iota((256, 128), 1) == 64 + 32 * (iota((256, 128), 0) // 128))
     second_hi = second_ref[:128]
     second_lo = second_ref[128:]
 
@@ -463,15 +466,17 @@
             ].astype(BF16)
             return carry
 
-        def pack_middle(d, carry):
-            z = stage[pl.ds(pl.multiple_of(d * 16, 16), 16), :]
-            at = jnp.full((16, 128), d, I32)
-            for p in range(2):
-                middle = jnp.take_along_axis(
-                    extra[p, group * 16 : group * 16 + 16, :], at, axis=1, mode="promise_in_bounds"
-                )
-                z = jnp.where(lane == 64 + 32 * p, middle, z)
-            out_ref[d, group * 16 : group * 16 + 16, :] = z.astype(BF16)
+        def pack_middle(d8, carry):
+            ahead = [extra[p, group * 16 : group * 16 + 16, :] for p in range(2)]
+            parts = []
+            for k in range(8):
+                mine = iota((16, 128), 1) == d8 * 8 + k
+                parts.append(jnp.concatenate([jnp.where(mine, z, 0.0) for z in ahead], axis=1))
+            more = dot(jnp.concatenate(parts, axis=0).astype(BF16), spots)
+            z = stage[pl.ds(pl.multiple_of(d8 * 128, 128), 128), :]
+            z = jnp.where((lane == 64) | (lane == 96), more, z).astype(BF16)
+            for k in range(8):
+                out_ref[d8 * 8 + k, group * 16 : group * 16 + 16, :] = z[16 * k : 16 * k + 16]
             return carry
 
         @pl.when(s != 0)
@@ -480,7 +485,7 @@
 
         @pl.when(s == 0)
         def _():
-            lax.fori_loop(0, 128, pack_middle, 0, unroll=8)
+            lax.fori_loop(0, 16, pack_middle, 0, unroll=8)
 
 
 def image_kernel(in_ref, first_ref, turn_ref, last_ref, out_ref, wide, left, right):
@@ -527,14 +532,14 @@
         hit = (final >= 0) & (first < 128 + TAPS - 1)
         one = (hit & (top >= first - (TAPS - 1))).astype(I32)
         two = (hit & (bottom <= final)).astype(I32)
-        both = one.reshape(128, NB_DEV) << shift | two.reshape(128, NB_DEV) << (shift + 16)
+        both = one << shift | two << (shift + 16)
         return jnp.sum(both, axis=1)
 
     direct = s * ROWS - row
     mirror = GRID - ROWS + 1 - s * ROWS - row
     middle = GRID // 2 - row
     middle = packed(middle, middle) * (s == 0).astype(I32)
-    return jnp.concatenate([packed(direct, direct + ROWS - 1), packed(mirror, mirror + ROWS - 1), middle])
+    return packed(direct, direct + ROWS - 1), packed(mirror, mirror + ROWS - 1), middle
 
 
 def gridded(words, codes_all, s, x_all, taps):
@@ -544,7 +549,7 @@
     return pl.pallas_call(
         grid_kernel,
         out_shape=jax.ShapeDtypeStruct((DEVICES, 64, 128), BF16),
-        in_specs=[smem] * 4 + [pl.BlockSpec(memory_space=pl.ANY)] * 2 + [vmem] * 3,
+        in_specs=[smem] * 6 + [pl.BlockSpec(memory_space=pl.ANY)] * 2 + [vmem] * 3,
         out_specs=vmem,
         scratch_shapes=[
             pltpu.VMEM((2, HEAD + GRID + 32, 128), F32),
@@ -561,7 +566,7 @@
         compiler_params=pltpu.CompilerParams(vmem_limit_bytes=60 * 1024 * 1024),
         name="grid_columns",
     )(
-        words, codes_all, jnp.asarray(bit_table()), s.reshape(1).astype(I32),
+        *words, codes_all.reshape(BLOCKS), jnp.asarray(bit_table()), s.reshape(1).astype(I32),
         x_all, jnp.asarray(first), taps, jnp.asarray(second), jnp.asarray(turn),
     )
 
@@ -610,7 +615,6 @@
     x_all = gathered(ordered).reshape(DEVICES, AGR, 128)
     found = x_all[:, NOTES : NOTES + 4, :NB_DEV].astype(I32)
     codes_all = ((found[:, 0] * 32 + found[:, 1]) << 14) | (found[:, 2] << 7) | found[:, 3]
-    codes_all = codes_all.reshape(BLOCKS)
     words = words_of(codes_all, s)
     taps = kernel_taps.transpose(1, 2, 0).reshape(2 * TAPS, 32)
     sent = gridded(words, codes_all, s, x_all, taps)

time: 137 us -> 132 us (0.964)
  blocking collectives: 52.6 us -> 47 us
    all_to_all x1, blocking collectives: 52.6 us -> 47 us  [shards(): got = lax.all_to_all(sent, BOTH, split_axis=0, concat_axis=0, tiled=True)]
where the time goes in v6:
time: 132 us
  Pallas kernels  80.4 us (61%)
  blocking collectives  47 us (36%)
  other arithmetic  3.51 us (3%)
    all_to_all x1, blocking collectives, shards(): got = lax.all_to_all(sent, BOTH, split_axis=0, concat_axis=0, tiled=True)  47 us
    pallas_call x1, Pallas kernels, gathered(): pl.pallas_call(gather_kernel, out_shape=jax.ShapeDtypeStruct((4, 4, 4, 2,...  33.4 us
    pallas_call x1, Pallas kernels, gridded(): pl.pallas_call(grid_kernel, out_shape=jax.ShapeDtypeStruct((DEVICES, 64,...  27.3 us
    pallas_call x1, Pallas kernels, imaged(): pl.pallas_call(image_kernel, out_shape=jax.ShapeDtypeStruct((2, 64, GRID)...  11.9 us
    pallas_call x1, Pallas kernels, sorted_blocks(): pl.pallas_call(sort_kernel, out_shape=jax.ShapeDtypeStruct((AGR, 128), BF...  7.69 us

profile of v6, /device:TPU:1, one launch (start us, length us, event | category | flops | bytes accessed | tf_op | source)
XLA Modules:
  0.0 132.1 jit_solution(3000628606314649599)
XLA Ops:
  0.0 7.7 %sort_blocks.1.x_ref = bf16[208,128]{1,0:T(8,128)(2,1)} custom-call(bf16[16,2,2,256]{3,2,1,0:T(2,128)(2,1)} %vis_ref.1, s32[16,256]{1,0:T(8,128)} %keep_ref.1, s32[16,256]{1,0:T(8,128)} %plane_ref.1, s32[16,256]{1,0:T(8,128)} %row_ref.1, s32[16,256]{1,0:T(8,128)} %col_ref.1, s32[16]{0:T(128)} %cell_ref.1, s32[16]{0:T(128)} %bitcast.47), custom_call_target="tpu_custom_call" | custom-call | tf_op jit(solution)/shard_map/sort_blocks/pallas_call | solution.py:600
  7.7 33.4 %gather_blocks.1 = bf16[4,4,4,2,208,128]{5,4,3,2,1,0:T(8,128)(2,1)} custom-call(bf16[208,128]{1,0:T(8,128)(2,1)} %sort_blocks.1.x_ref), custom_call_target="tpu_custom_call" | custom-call | tf_op jit(solution)/shard_map/gather_blocks/pallas_call | solution.py:236
  41.1 1.0 slice_convert_fusion
  42.2 0.5 broadcast.173
  42.7 1.0 fusion.11
  43.8 0.7 reshape.43.meta
  44.4 0.2 fusion
  44.6 0.8 fusion.4
  45.4 0.5 broadcast_multiply_fusion.words2
  45.9 27.3 %grid_columns.1 = bf16[128,64,128]{2,1,0:T(8,128)(2,1)} custom-call(s32[128]{0:T(128)} %get-tuple-element.6.words0, s32[128]{0:T(128)} %get-tuple-element.7.words1, s32[128]{0:T(128)} %broadcast_multiply_fusion.words2, s32[2048]{0:T(1024)} %reshape.43.meta, s32[32]{0:T(128)} %constant.68.clone.bits, s32[1]{0:T(128)} %bitcast.12.strip, ...), custom_call_target="tpu_custom_call" | custom-call | tf_op jit(solution)/shard_map/grid_columns/pallas_call | solution.py:549
  73.2 0.0 copy-start
  73.2 0.0 copy-start.1
  73.2 0.0 copy-start.2
  73.2 47.0 %all_to_all.5.in_ref = bf16[128,64,128]{2,1,0:T(8,128)(2,1)S(1)} all-to-all(bf16[128,64,128]{2,1,0:T(8,128)(2,1)} %grid_columns.1), channel_id=1, replica_groups=mesh['au'=16,'vert'=8] {'au','vert'}, dimensions={0} | all-to-all | bytes 4194304 | tf_op jit(solution)/shard_map/all_to_all | solution.py:621
  120.2 0.0 copy-done
  120.2 0.0 copy-done.1
  120.2 0.0 copy-done.2
  120.2 11.9 %image_rows.1 = f32[2,64,8192]{2,1,0:T(8,128)} custom-call(bf16[128,64,128]{2,1,0:T(8,128)(2,1)S(1)} %all_to_all.5.in_ref, bf16[256,256]{1,0:T(8,128)(2,1)S(1)} %copy-done.1, f32[3,256,128]{2,1,0:T(8,128)S(1)} %copy-done, bf16[64,256]{1,0:T(8,128)(2,1)S(1)} %copy-done.2), custom_call_target="tpu_custom_call" | custom-call | tf_op jit(solution)/shard_map/image_rows/pallas_call | solution.py:576
  (4 shorter events, 0.1 us)
Async XLA Ops:
  73.2 47.0 %copy-start = (f32[3,256,128]{2,1,0:T(8,128)S(1)}, f32[3,256,128]{2,1,0:T(8,128)}, u32[]{:S(2)}) copy-start(f32[3,256,128]{2,1,0:T(8,128)} %constant.73.clone.turn_ref) | copy-start | bytes 1179652
  73.2 47.0 %copy-start.1 = (bf16[256,256]{1,0:T(8,128)(2,1)S(1)}, bf16[256,256]{1,0:T(8,128)(2,1)}, u32[]{:S(2)}) copy-start(bf16[256,256]{1,0:T(8,128)(2,1)} %constant.72.clone.first_ref) | copy-start | bytes 393220
  73.2 47.0 %copy-start.2 = (bf16[64,256]{1,0:T(8,128)(2,1)S(1)}, bf16[64,256]{1,0:T(8,128)(2,1)}, u32[]{:S(2)}) copy-start(bf16[64,256]{1,0:T(8,128)(2,1)} %constant.74.clone.last_ref) | copy-start | bytes 98308

commit v7 on v6

--- a/solution.py
+++ b/solution.py
@@ -251,12 +251,11 @@
     return jnp.where(low, first, second)
 
 
-def placed(sources, tap, limit):
+def placed(sources, taps, limit):
     halves = [(source[:8], source[8:]) for source in sources]
     parts = [[] for _ in sources]
-    for i in range(tap.shape[0] // 8):
-        t = tap[8 * i : 8 * i + 8]
-        inside = (t >= 0) & (t < limit)
+    for t in taps:
+        inside = (t & -16) == 0 if limit is None else (t >= 0) & (t < limit)
         low = t < 8
         index = t & 7
         for out, pair in zip(parts, halves):
@@ -348,14 +347,19 @@
         base = jnp.where(middle, GRID // 2, jnp.where(mirror, GRID - s * ROWS, s * ROWS)) - anchor_row
         base = jnp.where(valid, base, -100000)
         least = jnp.where(mirror & (s == 0), 1, 0)
-        j = iota((ROWS, 128), 0)
         most = jnp.where(middle, 0, ROWS)
-        tap = jnp.where((j < least) | (j > most), -1, base + sign * j - row)
-        re0, re1, im0, im1 = placed(weights, tap, TAPS)
+        step = 8 * sign
+        j = iota((8, 128), 0)
+        ahead = jnp.where(mirror, -j, j)
+        tap = ahead + base - row
+        beyond = jnp.where(middle, -100000, 0)
+        tiles = [jnp.where((j < least) | (j > most), -1, tap)]
+        tiles += [tap + (step * i + beyond) for i in range(1, ROWS // 8)]
+        re0, re1, im0, im1 = placed(weights, tiles, None)
         left = jnp.concatenate([re0, re1, im0, im1], axis=0).astype(BF16)
         right = jnp.concatenate([-im0, -im1, re0, re1], axis=0).astype(BF16)
-        tap = jnp.where(mirror, 144, 0) + sign * iota((WINDOW, 128), 0) - col
-        col_re, col_im = placed(taps, tap, limit)
+        tap = ahead + jnp.where(mirror, 144, 0) - col
+        col_re, col_im = placed(taps, [tap + step * i for i in range(WINDOW // 8)], limit)
         cols = jnp.concatenate([col_re.astype(BF16), col_im.astype(BF16)], axis=1)
         patch = dot_nt(cols, jnp.concatenate([left, right], axis=1))
         start = jnp.where(mirror, GRID - 128 - anchor_col, anchor_col + HEAD)

time: 132 us -> 139 us (1.053)
  blocking collectives: 47 us -> 52.3 us
    all_to_all x1, blocking collectives: 47 us -> 52.3 us  [shards(): got = lax.all_to_all(sent, BOTH, split_axis=0, concat_axis=0, tiled=True)]
where the time goes in v7:
time: 139 us; the launch traced here: 138 us
  Pallas kernels  81.3 us (58%)
  blocking collectives  52.3 us (38%)
  other arithmetic  3.51 us (3%)
    all_to_all x1, blocking collectives, shards(): got = lax.all_to_all(sent, BOTH, split_axis=0, concat_axis=0, tiled=True)  52.3 us
    pallas_call x1, Pallas kernels, gathered(): pl.pallas_call(gather_kernel, out_shape=jax.ShapeDtypeStruct((4, 4, 4, 2,...  33.4 us
    pallas_call x1, Pallas kernels, gridded(): pl.pallas_call(grid_kernel, out_shape=jax.ShapeDtypeStruct((DEVICES, 64,...  28.2 us
    pallas_call x1, Pallas kernels, imaged(): pl.pallas_call(image_kernel, out_shape=jax.ShapeDtypeStruct((2, 64, GRID)...  11.9 us
    pallas_call x1, Pallas kernels, sorted_blocks(): pl.pallas_call(sort_kernel, out_shape=jax.ShapeDtypeStruct((AGR, 128), BF...  7.69 us

profile of v7, /device:TPU:1, one launch (start us, length us, event | category | flops | bytes accessed | tf_op | source)
XLA Modules:
  0.0 138.3 jit_solution(1875780593390388076)
XLA Ops:
  0.0 7.7 %sort_blocks.1.x_ref = bf16[208,128]{1,0:T(8,128)(2,1)} custom-call(bf16[16,2,2,256]{3,2,1,0:T(2,128)(2,1)} %vis_ref.1, s32[16,256]{1,0:T(8,128)} %keep_ref.1, s32[16,256]{1,0:T(8,128)} %plane_ref.1, s32[16,256]{1,0:T(8,128)} %row_ref.1, s32[16,256]{1,0:T(8,128)} %col_ref.1, s32[16]{0:T(128)} %cell_ref.1, s32[16]{0:T(128)} %bitcast.47), custom_call_target="tpu_custom_call" | custom-call | tf_op jit(solution)/shard_map/sort_blocks/pallas_call | solution.py:604
  7.7 33.4 %gather_blocks.1 = bf16[4,4,4,2,208,128]{5,4,3,2,1,0:T(8,128)(2,1)} custom-call(bf16[208,128]{1,0:T(8,128)(2,1)} %sort_blocks.1.x_ref), custom_call_target="tpu_custom_call" | custom-call | tf_op jit(solution)/shard_map/gather_blocks/pallas_call | solution.py:236
  41.1 1.0 slice_convert_fusion
  42.2 0.5 broadcast.173
  42.7 1.0 fusion.11
  43.8 0.7 reshape.43.meta
  44.4 0.2 fusion
  44.6 0.8 fusion.4
  45.4 0.5 broadcast_multiply_fusion.words2
  45.9 28.2 %grid_columns.1 = bf16[128,64,128]{2,1,0:T(8,128)(2,1)} custom-call(s32[128]{0:T(128)} %get-tuple-element.6.words0, s32[128]{0:T(128)} %get-tuple-element.7.words1, s32[128]{0:T(128)} %broadcast_multiply_fusion.words2, s32[2048]{0:T(1024)} %reshape.43.meta, s32[32]{0:T(128)} %constant.68.clone.bits, s32[1]{0:T(128)} %bitcast.12.strip, ...), custom_call_target="tpu_custom_call" | custom-call | tf_op jit(solution)/shard_map/grid_columns/pallas_call | solution.py:553
  74.1 0.0 copy-start
  74.1 0.0 copy-start.1
  74.1 0.0 copy-start.2
  74.2 52.3 %all_to_all.5.in_ref = bf16[128,64,128]{2,1,0:T(8,128)(2,1)S(1)} all-to-all(bf16[128,64,128]{2,1,0:T(8,128)(2,1)} %grid_columns.1), channel_id=1, replica_groups=mesh['au'=16,'vert'=8] {'au','vert'}, dimensions={0} | all-to-all | bytes 4194304 | tf_op jit(solution)/shard_map/all_to_all | solution.py:625
  126.4 0.0 copy-done
  126.4 0.0 copy-done.1
  126.4 0.0 copy-done.2
  126.4 11.9 %image_rows.1 = f32[2,64,8192]{2,1,0:T(8,128)} custom-call(bf16[128,64,128]{2,1,0:T(8,128)(2,1)S(1)} %all_to_all.5.in_ref, bf16[256,256]{1,0:T(8,128)(2,1)S(1)} %copy-done.1, f32[3,256,128]{2,1,0:T(8,128)S(1)} %copy-done, bf16[64,256]{1,0:T(8,128)(2,1)S(1)} %copy-done.2), custom_call_target="tpu_custom_call" | custom-call | tf_op jit(solution)/shard_map/image_rows/pallas_call | solution.py:580
  (4 shorter events, 0.1 us)
Async XLA Ops:
  74.1 52.3 %copy-start = (f32[3,256,128]{2,1,0:T(8,128)S(1)}, f32[3,256,128]{2,1,0:T(8,128)}, u32[]{:S(2)}) copy-start(f32[3,256,128]{2,1,0:T(8,128)} %constant.73.clone.turn_ref) | copy-start | bytes 1179652
  74.1 52.3 %copy-start.1 = (bf16[256,256]{1,0:T(8,128)(2,1)S(1)}, bf16[256,256]{1,0:T(8,128)(2,1)}, u32[]{:S(2)}) copy-start(bf16[256,256]{1,0:T(8,128)(2,1)} %constant.72.clone.first_ref) | copy-start | bytes 393220
  74.1 52.3 %copy-start.2 = (bf16[64,256]{1,0:T(8,128)(2,1)S(1)}, bf16[64,256]{1,0:T(8,128)(2,1)}, u32[]{:S(2)}) copy-start(bf16[64,256]{1,0:T(8,128)(2,1)} %constant.74.clone.last_ref) | copy-start | bytes 98308

commit v8 on v7

--- a/solution.py
+++ b/solution.py
@@ -186,24 +186,29 @@
         return made
 
     shared = []
-    for phase in range(2):
-        direct = []
-        for part, order in enumerate(ORDERS):
-            ref = region(part, order[:phase], here)
-            direct += [copy(ref, device(moved(order[phase], step), core)) for step in (2, 1, 3)]
-        for made in direct:
+
+    def sends(part, phase):
+        order = ORDERS[part]
+        ref = region(part, order[:phase], here)
+        return [copy(ref, device(moved(order[phase], step), core)) for step in (2, 1, 3)]
+
+    before = [sends(part, 0) for part in range(3)]
+    after = []
+    for part in range(3):
+        for made in before[part]:
             made.wait_recv()
+        after.append(sends(part, 1))
     for phase in (2,):
         plain, relayed = [], []
         for part, order in enumerate(ORDERS):
             full, dim = order[:phase], order[phase]
+            for made in after[part]:
+                made.wait_recv()
             ref = region(part, full, here)
             right = copy(ref, device(moved(dim, 1), core))
             left = copy(ref, device(moved(dim, 3), core))
             plain.append((right, left))
-        if phase == 2:
-            for part, order in enumerate(ORDERS):
-                shared.append(copy(region(part, order[:2], here), sibling))
+            shared.append(copy(ref, sibling))
         for part, order in enumerate(ORDERS):
             full, dim = order[:phase], order[phase]
             right, left = plain[part]

time: 139 us -> 134 us (0.964); the launches traced: 138 us -> 137 us
  blocking collectives: 52.3 us -> 50.2 us
    all_to_all x1, blocking collectives: 52.3 us -> 50.2 us  [shards(): got = lax.all_to_all(sent, BOTH, split_axis=0, concat_axis=0, tiled=True)]
where the time goes in v8:
time: 134 us; the launch traced here: 137 us
  Pallas kernels  81.9 us (61%)
  blocking collectives  50.2 us (37%)
  other arithmetic  3.51 us (3%)
    all_to_all x1, blocking collectives, shards(): got = lax.all_to_all(sent, BOTH, split_axis=0, concat_axis=0, tiled=True)  50.2 us
    pallas_call x1, Pallas kernels, gathered(): pl.pallas_call(gather_kernel, out_shape=jax.ShapeDtypeStruct((4, 4, 4, 2,...  34 us
    pallas_call x1, Pallas kernels, gridded(): pl.pallas_call(grid_kernel, out_shape=jax.ShapeDtypeStruct((DEVICES, 64,...  28.2 us
    pallas_call x1, Pallas kernels, imaged(): pl.pallas_call(image_kernel, out_shape=jax.ShapeDtypeStruct((2, 64, GRID)...  11.9 us
    pallas_call x1, Pallas kernels, sorted_blocks(): pl.pallas_call(sort_kernel, out_shape=jax.ShapeDtypeStruct((AGR, 128), BF...  7.69 us

profile of v8, /device:TPU:1, one launch (start us, length us, event | category | flops | bytes accessed | tf_op | source)
XLA Modules:
  0.0 136.9 jit_solution(15129140374243341416)
XLA Ops:
  0.0 7.7 %sort_blocks.1.x_ref = bf16[208,128]{1,0:T(8,128)(2,1)} custom-call(bf16[16,2,2,256]{3,2,1,0:T(2,128)(2,1)} %vis_ref.1, s32[16,256]{1,0:T(8,128)} %keep_ref.1, s32[16,256]{1,0:T(8,128)} %plane_ref.1, s32[16,256]{1,0:T(8,128)} %row_ref.1, s32[16,256]{1,0:T(8,128)} %col_ref.1, s32[16]{0:T(128)} %cell_ref.1, s32[16]{0:T(128)} %bitcast.47), custom_call_target="tpu_custom_call" | custom-call | tf_op jit(solution)/shard_map/sort_blocks/pallas_call | solution.py:609
  7.7 34.0 %gather_blocks.1 = bf16[4,4,4,2,208,128]{5,4,3,2,1,0:T(8,128)(2,1)} custom-call(bf16[208,128]{1,0:T(8,128)(2,1)} %sort_blocks.1.x_ref), custom_call_target="tpu_custom_call" | custom-call | tf_op jit(solution)/shard_map/gather_blocks/pallas_call | solution.py:241
  41.7 1.0 slice_convert_fusion
  42.8 0.5 broadcast.173
  43.3 1.0 fusion.11
  44.4 0.7 reshape.43.meta
  45.0 0.2 fusion
  45.2 0.8 fusion.4
  46.0 0.5 broadcast_multiply_fusion.words2
  46.5 28.2 %grid_columns.1 = bf16[128,64,128]{2,1,0:T(8,128)(2,1)} custom-call(s32[128]{0:T(128)} %get-tuple-element.6.words0, s32[128]{0:T(128)} %get-tuple-element.7.words1, s32[128]{0:T(128)} %broadcast_multiply_fusion.words2, s32[2048]{0:T(1024)} %reshape.43.meta, s32[32]{0:T(128)} %constant.68.clone.bits, s32[1]{0:T(128)} %bitcast.12.strip, ...), custom_call_target="tpu_custom_call" | custom-call | tf_op jit(solution)/shard_map/grid_columns/pallas_call | solution.py:558
  74.7 0.0 copy-start
  74.7 0.0 copy-start.1
  74.7 0.0 copy-start.2
  74.7 50.2 %all_to_all.5.in_ref = bf16[128,64,128]{2,1,0:T(8,128)(2,1)S(1)} all-to-all(bf16[128,64,128]{2,1,0:T(8,128)(2,1)} %grid_columns.1), channel_id=1, replica_groups=mesh['au'=16,'vert'=8] {'au','vert'}, dimensions={0} | all-to-all | bytes 4194304 | tf_op jit(solution)/shard_map/all_to_all | solution.py:630
  125.0 0.0 copy-done
  125.0 0.0 copy-done.1
  125.0 0.0 copy-done.2
  125.0 11.9 %image_rows.1 = f32[2,64,8192]{2,1,0:T(8,128)} custom-call(bf16[128,64,128]{2,1,0:T(8,128)(2,1)S(1)} %all_to_all.5.in_ref, bf16[256,256]{1,0:T(8,128)(2,1)S(1)} %copy-done.1, f32[3,256,128]{2,1,0:T(8,128)S(1)} %copy-done, bf16[64,256]{1,0:T(8,128)(2,1)S(1)} %copy-done.2), custom_call_target="tpu_custom_call" | custom-call | tf_op jit(solution)/shard_map/image_rows/pallas_call | solution.py:585
  (4 shorter events, 0.1 us)
Async XLA Ops:
  74.7 50.3 %copy-start = (f32[3,256,128]{2,1,0:T(8,128)S(1)}, f32[3,256,128]{2,1,0:T(8,128)}, u32[]{:S(2)}) copy-start(f32[3,256,128]{2,1,0:T(8,128)} %constant.73.clone.turn_ref) | copy-start | bytes 1179652
  74.7 50.3 %copy-start.1 = (bf16[256,256]{1,0:T(8,128)(2,1)S(1)}, bf16[256,256]{1,0:T(8,128)(2,1)}, u32[]{:S(2)}) copy-start(bf16[256,256]{1,0:T(8,128)(2,1)} %constant.72.clone.first_ref) | copy-start | bytes 393220
  74.7 50.3 %copy-start.2 = (bf16[64,256]{1,0:T(8,128)(2,1)S(1)}, bf16[64,256]{1,0:T(8,128)(2,1)}, u32[]{:S(2)}) copy-start(bf16[64,256]{1,0:T(8,128)(2,1)} %constant.74.clone.last_ref) | copy-start | bytes 98308
